TPU v7x, 128 devices: a whole 4x4x4 slice. The times are simulated.
128 devices in a mesh: row: 8 (over y, core), col: 16 (over x, z).
Axes of the slice: x: 4, y: 4, z: 4, core: 2. Of those that a mesh axis runs over, the one named last changes fastest.
Arguments:
- zvecs: float32 [8, 16, 48, 128, 128], P('row', 'col'), may hold values from -0.046875 to 0.046875
- coef: float32 [8, 16, 128, 128], P('row', 'col'), may hold values from 0.5 to 8
- blocks: float32 [8, 16, 8, 640, 640], P('row', 'col'), may hold values from -10 to 10
- send_idx: int32 [8, 16, 8, 640], P('row', 'col'), may hold values from 0 to 16383
- land_idx: int32 [8, 16, 8, 640], P('row', 'col'), may hold values from 0 to 16383
- active: int32 [8, 16, 8], P('row', 'col'), may hold values 0 or 1
- order: int32 [128], replicated, may hold values from 0 to 127, each once
Outputs:
- coarse: float32 [6144, 6144], P('row', 'col')
All inputs are finite; a program needn't handle non-finite values. No bound on the sum of `active` on one device may be relied on, other than what follows from the above.
Results may differ from a plain program's by a relative error of at most 0.0003.
Values sent between devices are 32-bit elements; how exact they have to be, the bound alone decides.
A program may use at most 128 MiB of HBM per device.

v0:
```python
import jax
import jax.numpy as jnp
from jax import lax
from jax.sharding import PartitionSpec as P

offsets_row = (-1, -1, -1, 0, 0, 1, 1, 1)
offsets_col = (-1, 0, 1, -1, 1, -1, 0, 1)


def extended(shard, sides, width):
    for axis, dim in sides:
        size, length = (lax.axis_size(axis), shard.shape[dim])
        up = [(i, (i + 1) % size) for i in range(size - 1)]
        down = [(j, i) for i, j in up]
        last = lax.slice_in_dim(shard, length - width, length, axis=dim)
        leading = lax.slice_in_dim(shard, 0, width, axis=dim)
        before = lax.ppermute(last, axis, up)
        after = lax.ppermute(leading, axis, down)
        shard = jnp.concatenate([before, shard, after], axis=dim)
    return shard


def local_image(zvec, coef):
    padded = jnp.pad(zvec, ((0, 0), (1, 1), (1, 1)))
    beside = padded[:, 2:, 1:-1] + padded[:, :-2, 1:-1] + padded[:, 1:-1, 2:] + padded[:, 1:-1, :-2]
    return (4.0 + coef) * zvec - beside


def on_device(zvecs, coef, blocks, send_idx, land_idx, active, order):
    zgrid = zvecs[0, 0]
    width = zgrid.shape[0]
    zflat = zgrid.reshape(width, -1)
    grid_row = lax.axis_index("row")
    grid_col = lax.axis_index("col")
    nrow = lax.axis_size("row")
    ncol = lax.axis_size("col")
    total = nrow * ncol
    everyone = jnp.arange(total, dtype=jnp.int32)
    step_row = jnp.array(offsets_row, jnp.int32)
    step_col = jnp.array(offsets_col, jnp.int32)
    to_row = grid_row + step_row
    to_col = grid_col + step_col
    send_ok = (
        (to_row >= 0) & (to_row < nrow) & (to_col >= 0) & (to_col < ncol) & (active[0, 0] == 1)
    )
    picked = jnp.take(zflat, send_idx[0, 0], axis=1)
    outgoing = jnp.einsum("knp,npq->nkq", picked, blocks[0, 0], precision=lax.Precision.HIGHEST)
    outgoing = outgoing * send_ok.astype(jnp.float32)[:, None, None]
    from_row = grid_row - step_row
    from_col = grid_col - step_col
    from_ok = (from_row >= 0) & (from_row < nrow) & (from_col >= 0) & (from_col < ncol)
    source = from_row * ncol + from_col
    beside_all = extended(outgoing[None, None], (("row", 0), ("col", 1)), 1)
    arrived = jnp.stack([beside_all[1 - offsets_row[n], 1 - offsets_col[n], n] for n in range(8)])
    landed = jnp.take(zflat, land_idx[0, 0], axis=1)
    pair = jnp.einsum("knp,nlp->nkl", landed, arrived, precision=lax.Precision.HIGHEST)
    image = local_image(zgrid, coef[0, 0])
    own = jnp.einsum("kxy,lxy->kl", zgrid, image, precision=lax.Precision.HIGHEST)
    allblocks = jnp.concatenate([own[None], pair], axis=0)
    myself = grid_row * ncol + grid_col
    own_id = jnp.sum(jnp.where(everyone == myself, order, 0))
    source_id = jnp.sum(jnp.where(source[:, None] == everyone[None, :], order[None, :], 0), axis=1)
    qids = jnp.concatenate([own_id[None], jnp.where(from_ok, source_id, -1)])
    select = (qids[:, None] == everyone[None, :]).astype(jnp.float32).reshape(9, ncol, nrow)
    strip = jnp.einsum("bcm,bkl->ckml", select, allblocks, precision=lax.Precision.HIGHEST)
    strip = strip.reshape(ncol, width, nrow * width)
    received = lax.all_to_all(strip, "col", split_axis=0, concat_axis=0, tiled=True)
    return received.reshape(ncol * width, nrow * width)


def solution(mesh):
    in_specs = (
        P("row", "col", None, None, None),
        P("row", "col", None, None),
        P("row", "col", None, None, None),
        P("row", "col", None, None),
        P("row", "col", None, None),
        P("row", "col", None),
        P(),
    )
    out_specs = P("row", "col")
    return jax.shard_map(
        on_device, mesh=mesh, in_specs=in_specs, out_specs=out_specs, check_vma=False
    )
```

profile of v0, /device:TPU:8, one launch (start us, length us, event | category | flops | bytes accessed | tf_op | source)
XLA Modules:
  0.0 166.9 jit_solution(16983023027587587286)
XLA Ops:
  2.2 6.7 %copy.23 = f32[1,1,48,128,128]{2,4,3,1,0:T(8,128)} copy(f32[1,1,48,128,128]{4,3,2,1,0:T(8,128)} %param.11) | data formatting | bytes 6291456 | tf_op args[0]
  8.9 16.8 %gather_fusion.1 = f32[5120,48]{1,0:T(8,128)S(1)} fusion(f32[48,16384]{0,1:T(8,128)} %bitcast.83, s32[5120]{0:T(1024)S(1)} %get-tuple-element.6), kind=kCustom, calls=%fused_computation.1.clone | custom fusion | bytes 1986560 | tf_op jit(solution)/shard_map/jit(_take)/gather | solution.py:46
  25.7 1.7 %copy.25 = f32[8,640,48]{1,2,0:T(8,128)} copy(f32[8,640,48]{2,1,0:T(8,128)S(1)} %bitcast.88) | data formatting | bytes 1966080 | tf_op jit(solution)/shard_map/jit(_take)/gather | solution.py:46
  27.5 10.7 %fusion.12 = f32[1,1,8,48,640]{4,3,2,1,0:T(8,128)S(1)} fusion(f32[1,1,8,640,640]{4,3,2,1,0:T(8,128)} %param.13, f32[8,640,48]{1,2,0:T(8,128)} %copy.25, f32[8]{0:T(128)S(1)} %fusion.42, pred[8,640]{1,0:T(8,128)(4,1)S(1)} %compare_and_fusion), kind=kOutput, calls=%fused_computation.18 | convolution fusion | flops 1887928320 | bytes 15078432 | tf_op jit(solution)/shard_map/knp,npq->nkq/dot_general | solution.py:47
  38.2 2.2 %collective-permute-start.1 = (f32[1,1,8,48,640]{4,3,2,1,0:T(8,128)S(1)}, f32[1,1,8,48,640]{4,3,2,1,0:T(8,128)S(1)}, u32[]{:S(2)}, u32[]{:S(2)}) collective-permute-start(f32[1,1,8,48,640]{4,3,2,1,0:T(8,128)S(1)} %fusion.12), channel_id=1, source_target_pairs={{16,0},{32,16},{48,32},{64,48},{80,64},{96,80},{112,96},{17,1},{33... | collective-permute-start | bytes 2949128 | tf_op jit(solution)/shard_map/ppermute | solution.py:18
  40.4 2.4 %collective-permute-start = (f32[1,1,8,48,640]{4,3,2,1,0:T(8,128)S(1)}, f32[1,1,8,48,640]{4,3,2,1,0:T(8,128)S(1)}, u32[]{:S(2)}, u32[]{:S(2)}) collective-permute-start(f32[1,1,8,48,640]{4,3,2,1,0:T(8,128)S(1)} %fusion.12), channel_id=1, source_target_pairs={{0,16},{16,32},{32,48},{48,64},{64,80},{80,96},{96,112},{1,17},{17... | collective-permute-start | bytes 2949128 | tf_op jit(solution)/shard_map/ppermute | solution.py:17
  42.8 9.2 %collective-permute-done.1 = f32[1,1,8,48,640]{4,3,2,1,0:T(8,128)S(1)} collective-permute-done((f32[1,1,8,48,640]{4,3,2,1,0:T(8,128)S(1)}, f32[1,1,8,48,640]{4,3,2,1,0:T(8,128)S(1)}, u32[]{:S(2)}, u32[]{:S(2)}) %collective-permute-start.1) | collective-permute-done | bytes 983072 | tf_op jit(solution)/shard_map/ppermute | solution.py:18
  52.0 3.8 %collective-permute-done = f32[1,1,8,48,640]{4,3,2,1,0:T(8,128)S(1)} collective-permute-done((f32[1,1,8,48,640]{4,3,2,1,0:T(8,128)S(1)}, f32[1,1,8,48,640]{4,3,2,1,0:T(8,128)S(1)}, u32[]{:S(2)}, u32[]{:S(2)}) %collective-permute-start) | collective-permute-done | bytes 983072 | tf_op jit(solution)/shard_map/ppermute | solution.py:17
  55.8 2.1 %pad_maximum_fusion = f32[3,1,8,48,640]{4,3,2,1,0:T(8,128)} fusion(f32[1,1,8,48,640]{4,3,2,1,0:T(8,128)S(1)} %collective-permute-done.1, f32[1,1,8,48,640]{4,3,2,1,0:T(8,128)S(1)} %fusion.12, f32[1,1,8,48,640]{4,3,2,1,0:T(8,128)S(1)} %collective-permute-done), kind=kLoop, calls=%fused_computation.15 | loop fusion | flops 1474560 | bytes 5898240 | tf_op jit(solution)/shard_map/concatenate | solution.py:19
  57.9 1.3 collective-permute-start.2
  59.2 6.2 %collective-permute-start.3 = (f32[3,1,8,48,640]{4,3,2,1,0:T(8,128)}, f32[3,1,8,48,640]{4,3,2,1,0:T(8,128)}, u32[]{:S(2)}, u32[]{:S(2)}) collective-permute-start(f32[3,1,8,48,640]{4,3,2,1,0:T(8,128)} %pad_maximum_fusion), channel_id=1, source_target_pairs={{0,1},{1,2},{2,3},{3,4},{4,5},{5,6},{6,7},{7,8},{8,9},{9,10},{10,1... | collective-permute-start | bytes 8847368 | tf_op jit(solution)/shard_map/ppermute | solution.py:17
  65.4 1.7 %fusion.5 = f32[48,128,128]{2,1,0:T(8,128)S(1)} fusion(f32[48,128,128]{2,1,0:T(8,128)S(1)} %bitcast.85, f32[128,128]{1,0:T(8,128)S(1)} %add_bitcast_fusion), kind=kLoop, calls=%fused_computation.11 | loop fusion | flops 3932160 | bytes 6356992 | tf_op jit(solution)/shard_map/sub | solution.py:26
  67.1 6.2 %fusion.15 = f32[1,48,48]{1,2,0:T(8,128)S(1)} fusion(f32[48,128,128]{2,1,0:T(8,128)S(1)} %bitcast.86, f32[48,128,128]{2,1,0:T(8,128)S(1)} %fusion.5), kind=kOutput, calls=%fused_computation.19 | convolution fusion | flops 452984832 | bytes 6300672 | tf_op jit(solution)/shard_map/kxy,lxy->kl/dot_general | solution.py:58
  73.4 16.8 %gather_fusion = f32[5120,48]{1,0:T(8,128)S(1)} fusion(f32[48,16384]{0,1:T(8,128)} %bitcast.84, s32[5120]{0:T(1024)S(1)} %get-tuple-element.7), kind=kCustom, calls=%fused_computation.clone | custom fusion | bytes 1986560 | tf_op jit(solution)/shard_map/jit(_take)/gather | solution.py:55
  90.3 1.8 %copy.24 = f32[8,640,48]{1,2,0:T(8,128)} copy(f32[8,640,48]{2,1,0:T(8,128)S(1)} %bitcast.87) | data formatting | bytes 1966080 | tf_op jit(solution)/shard_map/jit(_take)/gather | solution.py:55
  93.6 31.6 %collective-permute-done.2 = f32[3,1,8,48,640]{4,3,2,1,0:T(8,128)} collective-permute-done((f32[3,1,8,48,640]{4,3,2,1,0:T(8,128)}, f32[3,1,8,48,640]{4,3,2,1,0:T(8,128)}, u32[]{:S(2)}, u32[]{:S(2)}) %collective-permute-start.2) | collective-permute-done | bytes 2949152 | tf_op jit(solution)/shard_map/ppermute | solution.py:18
  127.0 0.9 fusion.35
  128.9 0.9 fusion.33
  132.5 2.4 %fusion.21 = f32[8,48,48]{2,1,0:T(8,128)S(1)} fusion(f32[8,48,640]{2,1,0:T(8,128)S(1)} %fusion.30, f32[8,640,48]{1,2,0:T(8,128)} %copy.24, pred[8,640]{1,0:T(8,128)(4,1)S(1)} %compare_and_fusion.1), kind=kOutput, calls=%fused_computation.21 | convolution fusion | flops 141803520 | bytes 2044928 | tf_op jit(solution)/shard_map/knp,nlp->nkl/dot_general | solution.py:56
  135.0 1.4 convolution_bitcast_fusion
  136.4 1.0 copy.28
  137.4 1.8 %reshape.39 = f32[16,48,384]{2,1,0:T(8,128)} reshape(f32[16,48,8,48]{3,2,1,0:T(8,128)S(1)} %copy.28) | data formatting | bytes 2359296 | tf_op jit(solution)/shard_map/reshape | solution.py:66
  139.2 26.7 %all_to_all.5 = f32[16,48,384]{2,1,0:T(8,128)S(1)} all-to-all(f32[16,48,384]{2,1,0:T(8,128)} %reshape.39), channel_id=1, replica_groups=mesh['row'=8,'col'=16] {'col'}, dimensions={0} | all-to-all | bytes 2359296 | tf_op jit(solution)/shard_map/all_to_all | solution.py:67
  165.9 1.0 copy.50
  (46 shorter events, 9.4 us)
Async XLA Ops:
  25.7 1.8 %copy-start.7 = (s32[1,1,8]{2,1,0:T(1,128)S(1)}, s32[1,1,8]{2,1,0:T(1,128)}, u32[]{:S(2)}) copy-start(s32[1,1,8]{2,1,0:T(1,128)} %param.16) | copy-start | bytes 100
  25.7 1.8 %copy-start.8 = (s32[8]{0:T(128)S(1)}, s32[8]{0:T(128)}, u32[]{:S(2)}) copy-start(s32[8]{0:T(128)} %constant.41.clone) | copy-start | bytes 100
  25.7 1.8 %copy-start.9 = (s32[8]{0:T(128)S(1)}, s32[8]{0:T(128)}, u32[]{:S(2)}) copy-start(s32[8]{0:T(128)} %constant.40.clone) | copy-start | bytes 100
  38.2 27.2 %copy-start.4 = (f32[1,1,128,128]{3,2,1,0:T(8,128)S(1)}, f32[1,1,128,128]{3,2,1,0:T(8,128)}, u32[]{:S(2)}) copy-start(f32[1,1,128,128]{3,2,1,0:T(8,128)} %param.12) | copy-start | bytes 196612
  38.2 27.2 %copy-start = (f32[1,1,48,128,128]{4,3,2,1,0:T(8,128)S(1)}, f32[1,1,48,128,128]{4,3,2,1,0:T(8,128)}, u32[]{:S(2)}) copy-start(f32[1,1,48,128,128]{4,3,2,1,0:T(8,128)} %param.11) | copy-start | bytes 9437188
  38.2 13.8 %collective-permute-start.1 = (f32[1,1,8,48,640]{4,3,2,1,0:T(8,128)S(1)}, f32[1,1,8,48,640]{4,3,2,1,0:T(8,128)S(1)}, u32[]{:S(2)}, u32[]{:S(2)}) collective-permute-start(f32[1,1,8,48,640]{4,3,2,1,0:T(8,128)S(1)} %fusion.12), channel_id=1, source_target_pairs={{16,0},{32,16},{48,32},{64,48},{80,64},{96,80},{112,96},{17,1},{33... | collective-permute-start | bytes 2949128 | tf_op jit(solution)/shard_map/ppermute | solution.py:18
  40.4 15.4 %collective-permute-start = (f32[1,1,8,48,640]{4,3,2,1,0:T(8,128)S(1)}, f32[1,1,8,48,640]{4,3,2,1,0:T(8,128)S(1)}, u32[]{:S(2)}, u32[]{:S(2)}) collective-permute-start(f32[1,1,8,48,640]{4,3,2,1,0:T(8,128)S(1)} %fusion.12), channel_id=1, source_target_pairs={{0,16},{16,32},{32,48},{48,64},{64,80},{80,96},{96,112},{1,17},{17... | collective-permute-start | bytes 2949128 | tf_op jit(solution)/shard_map/ppermute | solution.py:17
  52.0 7.2 %copy-start.2 = (f32[1,1,8,48,640]{4,3,2,1,0:T(8,128)}, f32[1,1,8,48,640]{4,3,2,1,0:T(8,128)S(1)}, u32[]{:S(2)}) copy-start(f32[1,1,8,48,640]{4,3,2,1,0:T(8,128)S(1)} %collective-permute-done.1) | copy-start | bytes 2949124
  55.8 2.1 %copy-start.1 = (f32[1,1,8,48,640]{4,3,2,1,0:T(8,128)}, f32[1,1,8,48,640]{4,3,2,1,0:T(8,128)S(1)}, u32[]{:S(2)}) copy-start(f32[1,1,8,48,640]{4,3,2,1,0:T(8,128)S(1)} %collective-permute-done) | copy-start | bytes 2949124
  57.9 67.3 %collective-permute-start.2 = (f32[3,1,8,48,640]{4,3,2,1,0:T(8,128)}, f32[3,1,8,48,640]{4,3,2,1,0:T(8,128)}, u32[]{:S(2)}, u32[]{:S(2)}) collective-permute-start(f32[3,1,8,48,640]{4,3,2,1,0:T(8,128)} %pad_maximum_fusion), channel_id=1, source_target_pairs={{1,0},{2,1},{3,2},{4,3},{5,4},{6,5},{7,6},{8,7},{9,8},{10,9},{11,1... | collective-permute-start | bytes 8847368 | tf_op jit(solution)/shard_map/ppermute | solution.py:18
  59.2 67.9 %collective-permute-start.3 = (f32[3,1,8,48,640]{4,3,2,1,0:T(8,128)}, f32[3,1,8,48,640]{4,3,2,1,0:T(8,128)}, u32[]{:S(2)}, u32[]{:S(2)}) collective-permute-start(f32[3,1,8,48,640]{4,3,2,1,0:T(8,128)} %pad_maximum_fusion), channel_id=1, source_target_pairs={{0,1},{1,2},{2,3},{3,4},{4,5},{5,6},{6,7},{7,8},{8,9},{9,10},{10,1... | collective-permute-start | bytes 8847368 | tf_op jit(solution)/shard_map/ppermute | solution.py:17
  90.2 1.8 %copy-start.10 = (s32[128]{0:T(128)S(1)}, s32[128]{0:T(128)}, u32[]{:S(2)}) copy-start(s32[128]{0:T(128)} %param.17) | copy-start | bytes 1540
  90.2 2.5 %copy-start.5 = (s32[8]{0:T(128)S(1)}, s32[8]{0:T(128)}, u32[]{:S(2)}) copy-start(s32[8]{0:T(128)} %constant.51) | copy-start | bytes 100
  90.2 2.4 %copy-start.6 = (s32[8]{0:T(128)S(1)}, s32[8]{0:T(128)}, u32[]{:S(2)}) copy-start(s32[8]{0:T(128)} %constant.50) | copy-start | bytes 100
  90.2 3.3 %copy-start.3 = (s32[1,1,8,640]{3,2,1,0:T(8,128)S(1)}, s32[1,1,8,640]{3,2,1,0:T(8,128)}, u32[]{:S(2)}) copy-start(s32[1,1,8,640]{3,2,1,0:T(8,128)} %param.15) | copy-start | bytes 61444
where the time goes:
time: 168 us; the launch traced here: 167 us
  local copies, waits for them, and re-layouts  55 us (33%)
  waiting for transfers between devices  44.6 us (27%)
  blocking collectives  26.7 us (16%)
  matrix products  20.7 us (12%)
  starting transfers between devices  12.1 us (7%)
  other arithmetic  7.57 us (5%)
    ppermute x2, waiting for transfers between devices, extended(): after = lax.ppermute(leading, axis, down)  40.8 us
    all_to_all x1, blocking collectives, on_device(): lax.all_to_all(strip, 'col', split_axis=0, concat_axis=0, tiled=True)  26.7 us
    gather x2, local copies, waits for them, and re-layouts, on_device(): landed = jnp.take(zflat, land_idx[0, 0], axis=1)  18.6 us
    gather x2, local copies, waits for them, and re-layouts, on_device(): picked = jnp.take(zflat, send_idx[0, 0], axis=1)  18.5 us
    unnamed x31, local copies, waits for them, and re-layouts  14.1 us
    dot_general x1, matrix products, on_device(): jnp.einsum('knp,npq->nkq', picked, blocks[0, 0], precision=lax.Precision....  10.7 us
    ppermute x2, starting transfers between devices, extended(): before = lax.ppermute(last, axis, up)  8.65 us
    dot_general x1, matrix products, on_device(): jnp.einsum('kxy,lxy->kl', zgrid, image, precision=lax.Precision.HIGHEST)  6.18 us
  transfers between devices with their start and end apart: 4, of which 3 were waited for; matrix products, arithmetic and copies ran while one was open for 18% of the time, Pallas kernels for 0%

commit v1 on v0

v1 whole, which is shorter than its diff:
```python
import functools

import jax
import jax.numpy as jnp
from jax import lax
from jax.experimental import pallas as pl
from jax.experimental.pallas import tpu as pltpu
from jax.sharding import PartitionSpec as P

f32 = jnp.float32
bf16 = jnp.bfloat16
MESH = pl.DeviceIdType.MESH

K = 48
CX = 128
ROWS = 640
NROW = 8
NCOL = 16
NX = 4
NZ = 4
PITCH = 136
CHUNKS = 4
PER = CX // CHUNKS
HALF = K // 2
WIDE = 8 * K
STEPS = ((-1, 1), (-1, -1), (0, 1), (0, -1), (1, 1), (1, -1), (-1, 0), (1, 0))
GROUPS = ((0, 3, (0, 1)), (3, 2, (6, 7)), (5, 2, (2, 3)), (7, 2, (4, 5)))
EMPTY = NX * 9


def split(x):
    high = x.astype(bf16)
    return high, (x - high.astype(f32)).astype(bf16)


def stacked(x):
    return jnp.concatenate(split(x), axis=0)


def unstack(product):
    return product[:K, :K] + product[K : 2 * K, :K] + product[:K, K : 2 * K]


def pair_step(t, odd):
    last = t // 3
    side = 1 - last
    dr = (t - 1) * side - last + 2 * last * odd
    dc = side - 2 * side * odd
    nine = (dr + 1) * 3 + dc + 1
    return dr, dc, nine - nine // 5


def gather_rows(cells, index, start, rows):
    for j in range(ROWS):
        rows[pl.ds(j, 1), :] = cells[pl.ds(index[start + j], 1), :]


def flipped(rows):
    return rows[...].astype(bf16).T[0 : 2 * K]


def times_block(rows, block, factor, out):
    picked = flipped(rows)
    for q0 in range(0, ROWS, 256):
        q1 = min(q0 + 256, ROWS)
        total, low_total = None, None
        for p0 in range(0, ROWS, 256):
            p1 = min(p0 + 256, ROWS)
            high, low = split(block[p0:p1, q0:q1])
            one = jnp.dot(picked[:, p0:p1], high, preferred_element_type=f32)
            two = jnp.dot(picked[0:K, p0:p1], low, preferred_element_type=f32)
            total = one if total is None else total + one
            low_total = two if low_total is None else low_total + two
        out[:, q0:q1] = (total[0:K] + total[K : 2 * K] + low_total) * factor


def assemble(
    remote,
    z_hbm, coef, blocks_hbm, send_hbm, land_hbm, active, order,
    strips_out, mask_out,
    zpad, cells, blocks, rows_a, rows_b, landed, sent, arrived, held, strips, received, pick_vec,
    send_idx, land_idx, pick,
    z_sem, block_sem, send_idx_sem, land_idx_sem, pick_sem,
    near_send, near_recv, x_send, x_recv, z_send, z_recv,
):
    row = lax.axis_index("row") if remote else 3
    col = lax.axis_index("col") if remote else 5
    x_me = col // NZ
    z_me = lax.rem(col, NZ)

    if remote:
        barrier = pltpu.get_barrier_semaphore()
        for dr, dc in STEPS:
            peer = (lax.rem(row + dr + NROW, NROW), lax.rem(col + dc + NCOL, NCOL))
            pl.semaphore_signal(barrier, inc=1, device_id=peer, device_id_type=MESH)
        for k in range(1, 4):
            peer = (row, lax.rem(col + NZ * k, NCOL))
            pl.semaphore_signal(barrier, inc=1, device_id=peer, device_id_type=MESH)
            peer = (row, x_me * NZ + lax.rem(z_me + k, NZ))
            pl.semaphore_signal(barrier, inc=1, device_id=peer, device_id_type=MESH)

    z_copies = [
        pltpu.make_async_copy(
            z_hbm.at[0, 0, :, pl.ds(i * PER, PER), :],
            zpad.at[pl.ds(0, K), pl.ds(8 + i * PER, PER), :],
            z_sem.at[i],
        )
        for i in range(CHUNKS)
    ]
    for copy in z_copies:
        copy.start()
    send_copies = [
        pltpu.make_async_copy(
            send_hbm.at[0, 0, n], send_idx.at[pl.ds(n * ROWS, ROWS)], send_idx_sem.at[n]
        )
        for n in range(8)
    ]
    for copy in send_copies:
        copy.start()
    block_copies = []
    for i, (dr, dc) in enumerate(STEPS):
        nine = (dr + 1) * 3 + dc + 1
        block_copies.append(
            pltpu.make_async_copy(
                blocks_hbm.at[0, 0, nine - nine // 5], blocks.at[i], block_sem.at[i]
            )
        )
        block_copies[-1].start()
    land_copies = [
        pltpu.make_async_copy(
            land_hbm.at[0, 0, n], land_idx.at[pl.ds(n * ROWS, ROWS)], land_idx_sem.at[n]
        )
        for n in range(8)
    ]
    for copy in land_copies:
        copy.start()

    lane = lax.broadcasted_iota(jnp.int32, (32, 128), 1)
    line = lax.broadcasted_iota(jnp.int32, (32, 128), 0)
    owner = order[...].reshape(1, 128)
    source = jnp.sum(
        jnp.where(owner == x_me * 32 + line, lane, 0), axis=1, keepdims=True
    )
    from_row = source // NCOL
    from_col = source - from_row * NCOL
    turn = (z_me - from_col + NCOL) % NZ
    dr = row - from_row
    dc = jnp.where(turn == 3, -1, turn)
    to_col = from_col + dc
    step = 2 * (dr + 1) + jnp.where(dc < 0, 1, 0)
    slot = jnp.where(
        dc == 0,
        jnp.where(dr == 0, 0, jnp.where(dr < 0, 3, 4)),
        1 + step + jnp.where(step >= 2, 2, 0),
    )
    good = (turn != 2) & (to_col >= 0) & (to_col < NCOL) & (dr >= -1) & (dr <= 1)
    place = jnp.where(good, (to_col // NZ) * 9 + slot, EMPTY)
    pick_vec[...] = jnp.broadcast_to(place, (32, 128))
    pick_copy = pltpu.make_async_copy(pick_vec, pick, pick_sem)
    pick_copy.start()

    lane8 = lax.broadcasted_iota(jnp.int32, (8, 128), 1)
    line8 = lax.broadcasted_iota(jnp.int32, (8, 128), 0)
    mine = jnp.sum(jnp.where(owner == col * 8 + line8, lane8, 0), axis=1, keepdims=True)
    at = lax.broadcasted_iota(jnp.int32, (8, WIDE), 1) // K
    here = at == lax.broadcasted_iota(jnp.int32, (8, WIDE), 0)
    mine = jnp.sum(jnp.where(here, jnp.broadcast_to(mine, (8, WIDE)), 0), axis=0, keepdims=True)
    mine_row = mine // NCOL
    mine_col = mine - mine_row * NCOL
    column = lax.broadcasted_iota(jnp.int32, (NCOL, WIDE), 0)
    near = (jnp.abs(mine_col - column) <= 1) & (jnp.abs(mine_row - row) <= 1)
    mask_out[...] = jnp.where(near, 1.0, 0.0)

    held[EMPTY] = jnp.zeros((HALF, 128), f32)
    for k in range(K + 1):
        zpad[k, 0:8, :] = jnp.zeros((8, 128), f32)
    zlines = zpad.reshape((K + 1) * PITCH, 128)

    eye = (
        lax.broadcasted_iota(jnp.int32, (128, 128), 0)
        == lax.broadcasted_iota(jnp.int32, (128, 128), 1)
    ).astype(bf16)

    def turn_chunk(i, carry):
        pltpu.make_async_copy(
            z_hbm.at[0, 0, :, pl.ds(i * PER, PER), :],
            zpad.at[pl.ds(0, K), pl.ds(8 + i * PER, PER), :],
            z_sem.at[i],
        ).wait()
        for u in range(PER):
            both = stacked(zlines[pl.ds(8 + i * PER + u, K, stride=PITCH), :])
            cells[pl.ds((i * PER + u) * 128, 128), 0 : 2 * K] = lax.dot_general(
                eye, both, (((1,), (1,)), ((), ())), preferred_element_type=f32
            )
        return carry

    lax.fori_loop(0, CHUNKS, turn_chunk, 0)

    for copy in send_copies:
        copy.wait()

    if remote:
        pl.semaphore_wait(barrier, 14)

    def near_copy(i, dr, dc):
        peer = (row + dr, col + dc)
        return pltpu.make_async_remote_copy(
            src_ref=sent.at[i],
            dst_ref=arrived.at[i],
            send_sem=near_send.at[i],
            recv_sem=near_recv.at[i],
            device_id=peer,
            device_id_type=MESH,
        )

    def inside(dr, dc):
        r, c = row + dr, col + dc
        return (r >= 0) & (r < NROW) & (c >= 0) & (c < NCOL)

    def send_step(t, odd, now, later):
        i = 2 * t + odd
        dr, dc, n = pair_step(t, odd)
        after = (i + 1) - (i + 1) // 8
        n_after = pair_step(after // 2, 1 - odd)[2]
        pltpu.make_async_copy(blocks_hbm.at[0, 0, n], blocks.at[i], block_sem.at[i]).wait()
        gather_rows(cells, send_idx, n_after * ROWS, later)
        keep = jnp.where(active[0, 0, n] == 1, 1.0, 0.0)
        times_block(now, blocks.at[i], keep, sent.at[i])
        if remote:
            @pl.when(inside(dr, dc))
            def _():
                near_copy(i, dr, dc).start()

    def send_two(t, carry):
        send_step(t, 0, rows_a, rows_b)
        send_step(t, 1, rows_b, rows_a)
        return carry

    gather_rows(cells, send_idx, pair_step(0, 0)[2] * ROWS, rows_a)
    lax.fori_loop(0, 4, send_two, 0)

    for copy in land_copies:
        copy.wait()

    first = lax.broadcasted_iota(jnp.int32, (K, 128), 1) == 0
    final = lax.broadcasted_iota(jnp.int32, (K, 128), 1) == 127

    def land_two(t, total):
        for odd, rows in ((0, rows_a), (1, rows_b)):
            gather_rows(cells, land_idx, pair_step(t, odd)[2] * ROWS, rows)
            landed[2 * t + odd] = flipped(rows)
        x0 = t * 32
        lines = [zlines[pl.ds(8 + x0 + u, K, stride=PITCH), :] for u in range(-1, 33)]
        for u in range(0, 32, 2):
            left, right = [], []
            for v in (u, u + 1):
                z = lines[v + 1]
                beside = lines[v] + lines[v + 2]
                beside += jnp.where(first, 0.0, pltpu.roll(z, 1, 1))
                beside += jnp.where(final, 0.0, pltpu.roll(z, 127, 1))
                image = (4.0 + coef[0, 0, pl.ds(x0 + v, 1), :]) * z - beside
                left.append(stacked(z))
                right.append(stacked(image))
            total = total + lax.dot_general(
                jnp.concatenate(left, axis=1),
                jnp.concatenate(right, axis=1),
                (((1,), (1,)), ((), ())),
                preferred_element_type=f32,
            )
        return total

    own = lax.fori_loop(0, 4, land_two, jnp.zeros((2 * K, 2 * K), f32))

    def put(slot, block):
        gap = jnp.zeros((HALF, 64 - K), f32)
        held[x_me * 9 + slot] = jnp.concatenate([block[:HALF], gap, block[HALF:], gap], axis=1)

    def x_copy(g, k):
        span = pl.ds(x_me * 9 + GROUPS[g][0], GROUPS[g][1])
        return pltpu.make_async_remote_copy(
            src_ref=held.at[span],
            dst_ref=held.at[span],
            send_sem=x_send.at[g * 3 + k - 1],
            recv_sem=x_recv.at[g * 3 + k - 1],
            device_id=(row, lax.rem(col + NZ * k, NCOL)),
            device_id_type=MESH,
        )

    put(0, unstack(own))
    for g, (slot, count, steps) in enumerate(GROUPS):
        slot = slot + count - 2
        for j, i in enumerate(steps):
            dr, dc = STEPS[i]
            if remote:
                @pl.when(inside(-dr, -dc))
                def _():
                    near_copy(i, dr, dc).wait_recv()
            there = stacked(arrived[i])
            put(slot + j, unstack(lax.dot_general(
                landed[i], there, (((1,), (1,)), ((), ())), preferred_element_type=f32
            )))
        if remote:
            for k in (2, 1, 3):
                x_copy(g, k).start()

    pick_copy.wait()
    if remote:
        for g in range(len(GROUPS)):
            for k in range(1, 4):
                x_copy(g, k).wait_recv()

    def z_copy(k):
        return pltpu.make_async_remote_copy(
            src_ref=strips.at[k],
            dst_ref=received.at[z_me],
            send_sem=z_send.at[k - 1],
            recv_sem=z_recv.at[k - 1],
            device_id=(row, x_me * NZ + lax.rem(z_me + k, NZ)),
            device_id_type=MESH,
        )

    for k in (2, 1, 3, 0):
        target = lax.rem(z_me + k, NZ)
        found = [held[pick[target * 8 + m, 0]] for m in range(8)]
        upper = jnp.concatenate([block[:, 0:K] for block in found], axis=1)
        lower = jnp.concatenate([block[:, 64 : 64 + K] for block in found], axis=1)
        strip = jnp.concatenate([upper, lower], axis=0)
        if k:
            strips[k] = strip
            if remote:
                z_copy(k).start()
        else:
            received[z_me] = strip

    if remote:
        for i, (dr, dc) in enumerate(STEPS):
            @pl.when(inside(dr, dc))
            def _():
                near_copy(i, dr, dc).wait_send()
        for g in range(len(GROUPS)):
            for k in range(1, 4):
                x_copy(g, k).wait_send()
        for k in range(1, 4):
            z_copy(k).wait_send()
        for k in range(1, 4):
            z_copy(k).wait_recv()
    strips_out[...] = received[...]


def place_strips(strips, mask, out):
    for p in range(NCOL):
        keep = mask[p : p + 1, :] > 0.5
        out[p * K : (p + 1) * K, :] = jnp.where(keep, strips[p % NZ], 0.0)


def assemble_call(remote, *args):
    vmem = pl.BlockSpec(memory_space=pltpu.VMEM)
    smem = pl.BlockSpec(memory_space=pltpu.SMEM)
    hbm = pl.BlockSpec(memory_space=pl.ANY)
    dma = pltpu.SemaphoreType.DMA
    return pl.pallas_call(
        functools.partial(assemble, remote),
        out_shape=(
            jax.ShapeDtypeStruct((NZ, K, WIDE), f32),
            jax.ShapeDtypeStruct((NCOL, WIDE), f32),
        ),
        in_specs=[hbm, vmem, hbm, hbm, hbm, smem, vmem],
        out_specs=(vmem, vmem),
        scratch_shapes=[
            pltpu.VMEM((K + 1, PITCH, 128), f32),
            pltpu.VMEM((CX * 128, 128), f32),
            pltpu.VMEM((8, ROWS, ROWS), f32),
            pltpu.VMEM((ROWS, 128), f32),
            pltpu.VMEM((ROWS, 128), f32),
            pltpu.VMEM((8, 2 * K, ROWS), bf16),
            pltpu.VMEM((8, K, ROWS), f32),
            pltpu.VMEM((8, K, ROWS), f32),
            pltpu.VMEM((EMPTY + 1, HALF, 128), f32),
            pltpu.VMEM((NZ, K, WIDE), f32),
            pltpu.VMEM((NZ, K, WIDE), f32),
            pltpu.VMEM((32, 128), jnp.int32),
            pltpu.SMEM((8 * ROWS,), jnp.int32),
            pltpu.SMEM((8 * ROWS,), jnp.int32),
            pltpu.SMEM((32, 128), jnp.int32),
            dma((CHUNKS,)), dma((8,)), dma((8,)), dma((8,)), dma,
            dma((8,)), dma((8,)), dma((12,)), dma((12,)), dma((3,)), dma((3,)),
        ],
        compiler_params=pltpu.CompilerParams(
            collective_id=0 if remote else None,
            has_side_effects=True,
            vmem_limit_bytes=56 * 2**20,
        ),
        cost_estimate=pl.CostEstimate(
            flops=2 * 10**9, bytes_accessed=18 * 10**6, transcendentals=0
        ),
    )(*args)


def on_device(zvecs, coef, blocks, send_idx, land_idx, active, order):
    strips, mask = assemble_call(True, zvecs, coef, blocks, send_idx, land_idx, active, order)
    return pl.pallas_call(
        place_strips,
        out_shape=jax.ShapeDtypeStruct((NCOL * K, WIDE), f32),
        in_specs=[pl.BlockSpec(memory_space=pltpu.VMEM)] * 2,
        out_specs=pl.BlockSpec(memory_space=pltpu.VMEM),
    )(strips, mask)


def solution(mesh):
    in_specs = (
        P("row", "col", None, None, None),
        P("row", "col", None, None),
        P("row", "col", None, None, None),
        P("row", "col", None, None),
        P("row", "col", None, None),
        P("row", "col", None),
        P(),
    )
    return jax.shard_map(
        on_device, mesh=mesh, in_specs=in_specs, out_specs=P("row", "col"), check_vma=False
    )
```

time: 168 us -> 41.1 us (0.24)
  local copies, waits for them, and re-layouts: 55 us -> 0 us
  waiting for transfers between devices: 44.6 us -> 0 us
  Pallas kernels: 0 us -> 40.7 us
  blocking collectives: 26.7 us -> 0 us
  matrix products: 20.7 us -> 0 us
  starting transfers between devices: 12.1 us -> 0 us
  other arithmetic: 7.57 us -> 0 us
    ppermute x4 -> x0, waiting for transfers between devices: 44.6 us -> none  [the longest x2 40.8 us: extended(): after = lax.ppermute(leading, axis, down)]
    pallas_call x0 -> x2, Pallas kernels: none -> 40.7 us  [the longest x1 38.6 us: assemble_call(): pl.pallas_call(functools.partial(assemble, remote), out_shape=(jax.ShapeD...]
    gather x4 -> x0, local copies, waits for them, and re-layouts: 37.1 us -> none  [the longest x2 18.6 us: on_device(): landed = jnp.take(zflat, land_idx[0, 0], axis=1)]
    all_to_all x1 -> x0, blocking collectives: 26.7 us -> none  [on_device(): lax.all_to_all(strip, 'col', split_axis=0, concat_axis=0, tiled=True)]
    dot_general x4 -> x0, matrix products: 20.7 us -> none  [the longest x1 10.7 us: on_device(): jnp.einsum('knp,npq->nkq', picked, blocks[0, 0], precision=lax.Precision....]
    unnamed x31 -> x0, local copies, waits for them, and re-layouts: 14.1 us -> none
    ppermute x4 -> x0, starting transfers between devices: 12.1 us -> none  [the longest x2 8.65 us: extended(): before = lax.ppermute(last, axis, up)]
    concatenate x3 -> x0, other arithmetic: 2.8 us -> none  [the longest x1 2.07 us: extended(): shard = jnp.concatenate([before, shard, after], axis=dim)]
  transfers between devices with their start and end apart: 4 -> 0, of which waited for: 3 -> 0; matrix products, arithmetic and copies ran while one was open for 18% -> 0% of each run, Pallas kernels for 0% -> 0%
where the time goes in v1:
time: 41.1 us; the launch traced here: 40.7 us
  Pallas kernels  40.7 us (99%)
    pallas_call x1, Pallas kernels, assemble_call(): pl.pallas_call(functools.partial(assemble, remote), out_shape=(jax.ShapeD...  38.6 us
    pallas_call x1, Pallas kernels, on_device(): pl.pallas_call(place_strips, out_shape=jax.ShapeDtypeStruct((NCOL * K, WI...  2.07 us

profile of v1, /device:TPU:8, one launch (start us, length us, event | category | flops | bytes accessed | tf_op | source)
XLA Modules:
  0.0 40.7 jit_solution(4689339167679676412)
XLA Ops:
  0.0 38.6 %shard_map.73 = (f32[4,48,384]{2,1,0:T(8,128)}, f32[16,384]{1,0:T(8,128)}) custom-call(f32[1,1,48,128,128]{4,3,2,1,0:T(8,128)} %z_hbm.1, f32[1,1,128,128]{3,2,1,0:T(8,128)} %coef.1, f32[1,1,8,640,640]{4,3,2,1,0:T(8,128)} %blocks_hbm.1, s32[1,1,8,640]{3,2,1,0:T(8,128)} %send_hbm.1, s32[1,1,8,640]{3,2,1,0:T(8,128)} %land_hbm.1, s32[1,1,8]{2,1,0:T(1,128)} %active.1, ...), custom_call_target="tpu_custom_call" | custom-call | flops 2000000000 | bytes 18000000 | tf_op jit(solution)/shard_map/pallas_call | solution.py:361
  38.6 2.1 %shard_map.74 = f32[768,384]{1,0:T(8,128)} custom-call(f32[4,48,384]{2,1,0:T(8,128)} %get-tuple-element.7.strips, f32[16,384]{1,0:T(8,128)} %get-tuple-element.8.mask), custom_call_target="tpu_custom_call" | custom-call | tf_op jit(solution)/shard_map/pallas_call | solution.py:401

commit v2 on v1

v2 whole, which is shorter than its diff:
```python
import functools

import jax
import jax.numpy as jnp
from jax import lax
from jax.experimental import pallas as pl
from jax.experimental.pallas import tpu as pltpu
from jax.sharding import PartitionSpec as P

f32 = jnp.float32
bf16 = jnp.bfloat16
MESH = pl.DeviceIdType.MESH

K = 48
CX = 128
ROWS = 640
NROW = 8
NCOL = 16
NX = 4
NZ = 4
HALVES = 2
PER = CX // HALVES
TURN = 32
HALF = K // 2
WIDE = 8 * K
STEPS = ((-1, 1), (-1, -1), (0, 1), (0, -1), (-1, 0), (1, 0), (1, 1), (1, -1))
FINISH = (0, 2, 1, 3)
EMPTY = NX * 9


def split(x):
    high = x.astype(bf16)
    return high, (x - high.astype(f32)).astype(bf16)


def stacked(x):
    return jnp.concatenate(split(x), axis=0)


def unstack(product):
    return product[:K, :K] + product[K : 2 * K, :K] + product[:K, K : 2 * K]


def pair_step(t, odd):
    up = t // 2 - t // 3
    dr = (t - 1 - t // 3) * (1 - up) + up * (2 * odd - 1)
    dc = (1 - up) * (1 - 2 * odd)
    nine = (dr + 1) * 3 + dc + 1
    return dr, dc, nine - nine // 5


def gather_rows(cells, index, start, rows):
    for j in range(ROWS):
        rows[pl.ds(j, 1), :] = cells[pl.ds(index[start + j], 1), :]


def flipped(rows):
    return rows[...].astype(bf16).T[0 : 2 * K]


def times_block(rows, block, factor, out):
    picked = flipped(rows)
    for q0 in range(0, ROWS, 256):
        q1 = min(q0 + 256, ROWS)
        total, low_total = None, None
        for p0 in range(0, ROWS, 256):
            p1 = min(p0 + 256, ROWS)
            high, low = split(block[p0:p1, q0:q1])
            one = jnp.dot(picked[:, p0:p1], high, preferred_element_type=f32)
            two = jnp.dot(picked[0:K, p0:p1], low, preferred_element_type=f32)
            total = one if total is None else total + one
            low_total = two if low_total is None else low_total + two
        out[:, q0:q1] = (total[0:K] + total[K : 2 * K] + low_total) * factor


def assemble(
    remote,
    z_hbm, coef, blocks_hbm, send_hbm, land_hbm, active, order,
    out,
    zlines, zparts, cells, blocks, rows_a, rows_b, landed, sent, arrived, held, strips, received,
    pick_vec, send_idx, land_idx, pick,
    z_sem, block_sem, send_idx_sem, land_idx_sem, pick_sem,
    near_send, near_recv, x_send, x_recv, z_send, z_recv,
):
    row = lax.axis_index("row") if remote else 3
    col = lax.axis_index("col") if remote else 5
    x_me = col // NZ
    z_me = lax.rem(col, NZ)

    def lines_of(half):
        return zlines.at[pl.ds(half * PER, PER)]

    for half in range(HALVES):
        for k in range(K):
            pltpu.make_async_copy(
                z_hbm.at[0, 0, k, pl.ds(half * PER, PER), :],
                zlines.at[pl.ds(half * PER, PER), k, :],
                z_sem.at[half],
            ).start()
    send_copies = [
        pltpu.make_async_copy(
            send_hbm.at[0, 0, n], send_idx.at[pl.ds(n * ROWS, ROWS)], send_idx_sem.at[n]
        )
        for n in range(8)
    ]
    for copy in send_copies:
        copy.start()
    for i, (dr, dc) in enumerate(STEPS):
        nine = (dr + 1) * 3 + dc + 1
        pltpu.make_async_copy(
            blocks_hbm.at[0, 0, nine - nine // 5], blocks.at[i], block_sem.at[i]
        ).start()
    land_copies = [
        pltpu.make_async_copy(
            land_hbm.at[0, 0, n], land_idx.at[pl.ds(n * ROWS, ROWS)], land_idx_sem.at[n]
        )
        for n in range(8)
    ]
    for copy in land_copies:
        copy.start()

    if remote:
        barrier = pltpu.get_barrier_semaphore()
        for dr, dc in STEPS:
            peer = (lax.rem(row + dr + NROW, NROW), lax.rem(col + dc + NCOL, NCOL))
            pl.semaphore_signal(barrier, inc=1, device_id=peer, device_id_type=MESH)
        for k in range(1, 4):
            peer = (row, lax.rem(col + NZ * k, NCOL))
            pl.semaphore_signal(barrier, inc=1, device_id=peer, device_id_type=MESH)
            peer = (row, x_me * NZ + lax.rem(z_me + k, NZ))
            pl.semaphore_signal(barrier, inc=1, device_id=peer, device_id_type=MESH)

    zlines[CX] = jnp.zeros((K, 128), f32)
    eye = (
        lax.broadcasted_iota(jnp.int32, (128, 128), 0)
        == lax.broadcasted_iota(jnp.int32, (128, 128), 1)
    ).astype(bf16)

    def turn_chunk(i, carry):
        for u in range(TURN):
            both = stacked(zlines[i * TURN + u])
            zparts[i * TURN + u] = both
            cells[pl.ds((i * TURN + u) * 128, 128), 0 : 2 * K] = lax.dot_general(
                eye, both, (((1,), (1,)), ((), ())), preferred_element_type=f32
            )
        return carry

    for half in range(HALVES):
        pltpu.make_async_copy(lines_of(half), lines_of(half), z_sem.at[half]).wait()
        lax.fori_loop(half * PER // TURN, (half + 1) * PER // TURN, turn_chunk, 0)

    for copy in send_copies:
        copy.wait()

    if remote:
        pl.semaphore_wait(barrier, 14)

    def near_copy(i, dr, dc):
        peer = (row + dr, col + dc)
        return pltpu.make_async_remote_copy(
            src_ref=sent.at[i],
            dst_ref=arrived.at[i],
            send_sem=near_send.at[i],
            recv_sem=near_recv.at[i],
            device_id=peer,
            device_id_type=MESH,
        )

    def inside(dr, dc):
        r, c = row + dr, col + dc
        return (r >= 0) & (r < NROW) & (c >= 0) & (c < NCOL)

    def send_step(t, odd, now, later):
        i = 2 * t + odd
        dr, dc, n = pair_step(t, odd)
        after = (i + 1) - (i + 1) // 8
        n_after = pair_step(after // 2, 1 - odd)[2]
        pltpu.make_async_copy(blocks_hbm.at[0, 0, n], blocks.at[i], block_sem.at[i]).wait()
        gather_rows(cells, send_idx, n_after * ROWS, later)
        keep = jnp.where(active[0, 0, n] == 1, 1.0, 0.0)
        times_block(now, blocks.at[i], keep, sent.at[i])
        if remote:
            @pl.when(inside(dr, dc))
            def _():
                near_copy(i, dr, dc).start()

    def send_two(t, carry):
        send_step(t, 0, rows_a, rows_b)
        send_step(t, 1, rows_b, rows_a)
        return carry

    gather_rows(cells, send_idx, pair_step(0, 0)[2] * ROWS, rows_a)
    lax.fori_loop(0, 4, send_two, 0)

    lane = lax.broadcasted_iota(jnp.int32, (32, 128), 1)
    line = lax.broadcasted_iota(jnp.int32, (32, 128), 0)
    owner = order[...].reshape(1, 128)
    source = jnp.sum(
        jnp.where(owner == x_me * 32 + line, lane, 0), axis=1, keepdims=True
    )
    from_row = source // NCOL
    from_col = source - from_row * NCOL
    turn = (z_me - from_col + NCOL) % NZ
    dr = row - from_row
    dc = jnp.where(turn == 3, -1, turn)
    to_col = from_col + dc
    step = 2 * (dr + 1) + jnp.where(dc < 0, 1, 0)
    slot = jnp.where(
        dc == 0,
        jnp.where(dr == 0, 0, jnp.where(dr < 0, 5, 6)),
        1 + step + jnp.where(dr > 0, 2, 0),
    )
    good = (turn != 2) & (to_col >= 0) & (to_col < NCOL) & (dr >= -1) & (dr <= 1)
    place = jnp.where(good, (to_col // NZ) * 9 + slot, EMPTY)
    pick_vec[...] = jnp.broadcast_to(place, (32, 128))
    pick_copy = pltpu.make_async_copy(pick_vec, pick, pick_sem)
    pick_copy.start()

    lane8 = lax.broadcasted_iota(jnp.int32, (8, 128), 1)
    line8 = lax.broadcasted_iota(jnp.int32, (8, 128), 0)
    mine = jnp.sum(jnp.where(owner == col * 8 + line8, lane8, 0), axis=1, keepdims=True)
    at = lax.broadcasted_iota(jnp.int32, (8, WIDE), 1) // K
    here = at == lax.broadcasted_iota(jnp.int32, (8, WIDE), 0)
    mine = jnp.sum(jnp.where(here, jnp.broadcast_to(mine, (8, WIDE)), 0), axis=0, keepdims=True)
    mine_row = mine // NCOL
    mine_col = mine - mine_row * NCOL
    column = lax.broadcasted_iota(jnp.int32, (NCOL, WIDE), 0)
    near = (jnp.abs(mine_col - column) <= 1) & (jnp.abs(mine_row - row) <= 1)

    held[EMPTY] = jnp.zeros((HALF, 128), f32)

    for copy in land_copies:
        copy.wait()

    final = lax.broadcasted_iota(jnp.int32, (K, 128), 1) == 127

    def land_two(t, total):
        for odd in (0, 1):
            gather_rows(cells, land_idx, pair_step(t, odd)[2] * ROWS, landed.at[2 * t + odd])
        x0 = t * 32
        left, right = [], []
        for v in range(32):
            z = zlines[x0 + v]
            beside = zlines[x0 + v + 1] + jnp.where(final, 0.0, pltpu.roll(z, 127, 1))
            half_image = (2.0 + 0.5 * coef[0, 0, pl.ds(x0 + v, 1), :]) * z - beside
            left.append(zparts[x0 + v])
            right.append(stacked(half_image))
        return total + lax.dot_general(
            jnp.concatenate(left, axis=1),
            jnp.concatenate(right, axis=1),
            (((1,), (1,)), ((), ())),
            preferred_element_type=f32,
        )

    own = unstack(lax.fori_loop(0, 4, land_two, jnp.zeros((2 * K, 2 * K), f32)))
    own = own + own.T

    def put(slot, block):
        gap = jnp.zeros((HALF, 64 - K), f32)
        held[x_me * 9 + slot] = jnp.concatenate([block[:HALF], gap, block[HALF:], gap], axis=1)

    def x_copy(t, k):
        span = pl.ds(x_me * 9 + (2 * t + 1 if t else 0), 2 if t else 3)
        return pltpu.make_async_remote_copy(
            src_ref=held.at[span],
            dst_ref=held.at[span],
            send_sem=x_send.at[t * 3 + k - 1],
            recv_sem=x_recv.at[t * 3 + k - 1],
            device_id=(row, lax.rem(col + NZ * k, NCOL)),
            device_id_type=MESH,
        )

    put(0, own)
    for t in FINISH:
        for i in (2 * t, 2 * t + 1):
            dr, dc = STEPS[i]
            if remote:
                @pl.when(inside(-dr, -dc))
                def _():
                    near_copy(i, dr, dc).wait_recv()
            product = jnp.dot(
                stacked(arrived[i]), landed[i].astype(bf16), preferred_element_type=f32
            )
            put(i + 1, unstack(product.T))
        if remote:
            for k in (2, 1, 3):
                x_copy(t, k).start()

    pick_copy.wait()
    if remote:
        for g in range(4):
            for k in range(1, 4):
                x_copy(g, k).wait_recv()

    def z_copy(k):
        return pltpu.make_async_remote_copy(
            src_ref=strips.at[k],
            dst_ref=received.at[z_me],
            send_sem=z_send.at[k - 1],
            recv_sem=z_recv.at[k - 1],
            device_id=(row, x_me * NZ + lax.rem(z_me + k, NZ)),
            device_id_type=MESH,
        )

    for k in (2, 1, 3, 0):
        target = lax.rem(z_me + k, NZ)
        found = [held[pick[target * 8 + m, 0]] for m in range(8)]
        upper = jnp.concatenate([block[:, 0:K] for block in found], axis=1)
        lower = jnp.concatenate([block[:, 64 : 64 + K] for block in found], axis=1)
        strip = jnp.concatenate([upper, lower], axis=0)
        if k:
            strips[k] = strip
            if remote:
                z_copy(k).start()
        else:
            received[z_me] = strip

    if remote:
        for i, (dr, dc) in enumerate(STEPS):
            @pl.when(inside(dr, dc))
            def _():
                near_copy(i, dr, dc).wait_send()
        for g in range(4):
            for k in range(1, 4):
                x_copy(g, k).wait_send()
        for k in range(1, 4):
            z_copy(k).wait_send()
        for k in range(1, 4):
            z_copy(k).wait_recv()
    for p in range(NCOL):
        out[p * K : (p + 1) * K, :] = jnp.where(near[p : p + 1, :], received[p % NZ], 0.0)


def assemble_call(remote, *args):
    vmem = pl.BlockSpec(memory_space=pltpu.VMEM)
    smem = pl.BlockSpec(memory_space=pltpu.SMEM)
    hbm = pl.BlockSpec(memory_space=pl.ANY)
    dma = pltpu.SemaphoreType.DMA
    return pl.pallas_call(
        functools.partial(assemble, remote),
        out_shape=jax.ShapeDtypeStruct((NCOL * K, WIDE), f32),
        in_specs=[hbm, vmem, hbm, hbm, hbm, smem, vmem],
        out_specs=vmem,
        scratch_shapes=[
            pltpu.VMEM((CX + 1, K, 128), f32),
            pltpu.VMEM((CX, 2 * K, 128), bf16),
            pltpu.VMEM((CX * 128, 128), f32),
            pltpu.VMEM((8, ROWS, ROWS), f32),
            pltpu.VMEM((ROWS, 128), f32),
            pltpu.VMEM((ROWS, 128), f32),
            pltpu.VMEM((8, ROWS, 128), f32),
            pltpu.VMEM((8, K, ROWS), f32),
            pltpu.VMEM((8, K, ROWS), f32),
            pltpu.VMEM((EMPTY + 1, HALF, 128), f32),
            pltpu.VMEM((NZ, K, WIDE), f32),
            pltpu.VMEM((NZ, K, WIDE), f32),
            pltpu.VMEM((32, 128), jnp.int32),
            pltpu.SMEM((8 * ROWS,), jnp.int32),
            pltpu.SMEM((8 * ROWS,), jnp.int32),
            pltpu.SMEM((32, 128), jnp.int32),
            dma((HALVES,)), dma((8,)), dma((8,)), dma((8,)), dma,
            dma((8,)), dma((8,)), dma((12,)), dma((12,)), dma((3,)), dma((3,)),
        ],
        compiler_params=pltpu.CompilerParams(
            collective_id=0 if remote else None,
            has_side_effects=True,
            vmem_limit_bytes=56 * 2**20,
        ),
        cost_estimate=pl.CostEstimate(
            flops=2 * 10**9, bytes_accessed=18 * 10**6, transcendentals=0
        ),
    )(*args)


def on_device(zvecs, coef, blocks, send_idx, land_idx, active, order):
    return assemble_call(True, zvecs, coef, blocks, send_idx, land_idx, active, order)


def solution(mesh):
    in_specs = (
        P("row", "col", None, None, None),
        P("row", "col", None, None),
        P("row", "col", None, None, None),
        P("row", "col", None, None),
        P("row", "col", None, None),
        P("row", "col", None),
        P(),
    )
    return jax.shard_map(
        on_device, mesh=mesh, in_specs=in_specs, out_specs=P("row", "col"), check_vma=False
    )
```

time: 41.1 us -> 40.3 us (0.981)
  Pallas kernels: 40.7 us -> 37.6 us
  local copies, waits for them, and re-layouts: 0 us -> 2.36 us
    pallas_call x2 -> x1, Pallas kernels: 40.7 us -> 37.6 us  [assemble_call(): pl.pallas_call(functools.partial(assemble, remote), out_shape=jax.ShapeDt...]
    unnamed x0 -> x1, local copies, waits for them, and re-layouts: none -> 2.36 us
where the time goes in v2:
time: 40.3 us; the launch traced here: 40 us
  Pallas kernels  37.6 us (93%)
  local copies, waits for them, and re-layouts  2.36 us (6%)
    pallas_call x1, Pallas kernels, assemble_call(): pl.pallas_call(functools.partial(assemble, remote), out_shape=jax.ShapeDt...  37.6 us
    unnamed x1, local copies, waits for them, and re-layouts  2.36 us

profile of v2, /device:TPU:8, one launch (start us, length us, event | category | flops | bytes accessed | tf_op | source)
XLA Modules:
  0.0 40.0 jit_solution(6061341297514999783)
XLA Ops:
  0.0 37.6 %shard_map.73 = f32[768,384]{1,0:T(8,128)} custom-call(f32[1,1,48,128,128]{4,3,2,1,0:T(8,128)} %z_hbm.1, f32[1,1,128,128]{3,2,1,0:T(8,128)} %coef.1, f32[1,1,8,640,640]{4,3,2,1,0:T(8,128)} %blocks_hbm.1, s32[1,1,8,640]{3,2,1,0:T(8,128)} %send_hbm.1, s32[1,1,8,640]{3,2,1,0:T(8,128)} %land_hbm.1, s32[1,1,8]{2,1,0:T(1,128)} %active.1, s32[128]{0:T(128)} %order.1), custom_call_target="tpu_custom_call" | custom-call | flops 2000000000 | bytes 18000000 | tf_op jit(solution)/shard_map/pallas_call | solution.py:339
  37.6 2.4 %copy.9 = f32[768,384]{1,0:T(8,128)} copy(f32[768,384]{1,0:T(8,128)} %shard_map.73) | data formatting | bytes 2359296

commit v3 on v2

--- a/solution.py
+++ b/solution.py
@@ -24,7 +24,9 @@
 HALF = K // 2
 WIDE = 8 * K
 STEPS = ((-1, 1), (-1, -1), (0, 1), (0, -1), (-1, 0), (1, 0), (1, 1), (1, -1))
-FINISH = (0, 2, 1, 3)
+GROUPS = ((0, 2), (2, 2), (4, 3), (7, 2))
+SLOTS = (0, 1, 5, 6, 2, 3, 7, 8)
+OWN_SLOT = 4
 EMPTY = NX * 9
 
 
@@ -41,25 +43,17 @@
     return product[:K, :K] + product[K : 2 * K, :K] + product[:K, K : 2 * K]
 
 
-def pair_step(t, odd):
-    up = t // 2 - t // 3
-    dr = (t - 1 - t // 3) * (1 - up) + up * (2 * odd - 1)
-    dc = (1 - up) * (1 - 2 * odd)
-    nine = (dr + 1) * 3 + dc + 1
-    return dr, dc, nine - nine // 5
-
-
-def gather_rows(cells, index, start, rows):
+def direction(i):
+    nine = (STEPS[i][0] + 1) * 3 + STEPS[i][1] + 1
+    return nine - nine // 5
+
+
+def gather_rows(cells, index, n, rows):
     for j in range(ROWS):
-        rows[pl.ds(j, 1), :] = cells[pl.ds(index[start + j], 1), :]
-
-
-def flipped(rows):
-    return rows[...].astype(bf16).T[0 : 2 * K]
-
-
-def times_block(rows, block, factor, out):
-    picked = flipped(rows)
+        rows[pl.ds(j, 1), :] = cells[pl.ds(index[n, j], 1), :]
+
+
+def times_block(picked, block, factor, out):
     for q0 in range(0, ROWS, 256):
         q1 = min(q0 + 256, ROWS)
         total, low_total = None, None
@@ -76,8 +70,9 @@
 def assemble(
     remote,
     z_hbm, coef, blocks_hbm, send_hbm, land_hbm, active, order,
-    out,
-    zlines, zparts, cells, blocks, rows_a, rows_b, landed, sent, arrived, held, strips, received,
+    strips_out, mask_out,
+    zlines, zparts, cells, blocks, rows_a, rows_b, picked_a, picked_b, landed, sent, arrived,
+    held, strips, received,
     pick_vec, send_idx, land_idx, pick,
     z_sem, block_sem, send_idx_sem, land_idx_sem, pick_sem,
     near_send, near_recv, x_send, x_recv, z_send, z_recv,
@@ -97,27 +92,16 @@
                 zlines.at[pl.ds(half * PER, PER), k, :],
                 z_sem.at[half],
             ).start()
-    send_copies = [
-        pltpu.make_async_copy(
-            send_hbm.at[0, 0, n], send_idx.at[pl.ds(n * ROWS, ROWS)], send_idx_sem.at[n]
-        )
-        for n in range(8)
+    send_copy = pltpu.make_async_copy(send_hbm.at[0, 0], send_idx, send_idx_sem)
+    send_copy.start()
+    block_copies = [
+        pltpu.make_async_copy(blocks_hbm.at[0, 0, direction(i)], blocks.at[i], block_sem.at[i])
+        for i in range(8)
     ]
-    for copy in send_copies:
+    for copy in block_copies:
         copy.start()
-    for i, (dr, dc) in enumerate(STEPS):
-        nine = (dr + 1) * 3 + dc + 1
-        pltpu.make_async_copy(
-            blocks_hbm.at[0, 0, nine - nine // 5], blocks.at[i], block_sem.at[i]
-        ).start()
-    land_copies = [
-        pltpu.make_async_copy(
-            land_hbm.at[0, 0, n], land_idx.at[pl.ds(n * ROWS, ROWS)], land_idx_sem.at[n]
-        )
-        for n in range(8)
-    ]
-    for copy in land_copies:
-        copy.start()
+    land_copy = pltpu.make_async_copy(land_hbm.at[0, 0], land_idx, land_idx_sem)
+    land_copy.start()
 
     if remote:
         barrier = pltpu.get_barrier_semaphore()
@@ -131,26 +115,18 @@
             pl.semaphore_signal(barrier, inc=1, device_id=peer, device_id_type=MESH)
 
     zlines[CX] = jnp.zeros((K, 128), f32)
-    eye = (
-        lax.broadcasted_iota(jnp.int32, (128, 128), 0)
-        == lax.broadcasted_iota(jnp.int32, (128, 128), 1)
-    ).astype(bf16)
-
     def turn_chunk(i, carry):
         for u in range(TURN):
             both = stacked(zlines[i * TURN + u])
             zparts[i * TURN + u] = both
-            cells[pl.ds((i * TURN + u) * 128, 128), 0 : 2 * K] = lax.dot_general(
-                eye, both, (((1,), (1,)), ((), ())), preferred_element_type=f32
-            )
+            cells[pl.ds((i * TURN + u) * 128, 128), 0 : 2 * K] = both.T.astype(f32)
         return carry
 
     for half in range(HALVES):
         pltpu.make_async_copy(lines_of(half), lines_of(half), z_sem.at[half]).wait()
         lax.fori_loop(half * PER // TURN, (half + 1) * PER // TURN, turn_chunk, 0)
 
-    for copy in send_copies:
-        copy.wait()
+    send_copy.wait()
 
     if remote:
         pl.semaphore_wait(barrier, 14)
@@ -170,27 +146,37 @@
         r, c = row + dr, col + dc
         return (r >= 0) & (r < NROW) & (c >= 0) & (c < NCOL)
 
-    def send_step(t, odd, now, later):
-        i = 2 * t + odd
-        dr, dc, n = pair_step(t, odd)
-        after = (i + 1) - (i + 1) // 8
-        n_after = pair_step(after // 2, 1 - odd)[2]
-        pltpu.make_async_copy(blocks_hbm.at[0, 0, n], blocks.at[i], block_sem.at[i]).wait()
-        gather_rows(cells, send_idx, n_after * ROWS, later)
-        keep = jnp.where(active[0, 0, n] == 1, 1.0, 0.0)
-        times_block(now, blocks.at[i], keep, sent.at[i])
+    rows = (rows_a, rows_b)
+    picked = (picked_a, picked_b)
+
+    def pick_up(i):
+        gather_rows(cells, send_idx, direction(i), rows[i % 2])
+
+    def flip(i):
+        picked[i % 2][...] = rows[i % 2][...].astype(bf16).T[0 : 2 * K]
+
+    def multiply(i):
+        block_copies[i].wait()
+        keep = jnp.where(active[0, 0, direction(i)] == 1, 1.0, 0.0)
+        times_block(picked[i % 2], blocks.at[i], keep, sent.at[i])
         if remote:
+            dr, dc = STEPS[i]
+
             @pl.when(inside(dr, dc))
             def _():
                 near_copy(i, dr, dc).start()
 
-    def send_two(t, carry):
-        send_step(t, 0, rows_a, rows_b)
-        send_step(t, 1, rows_b, rows_a)
-        return carry
-
-    gather_rows(cells, send_idx, pair_step(0, 0)[2] * ROWS, rows_a)
-    lax.fori_loop(0, 4, send_two, 0)
+    pick_up(0)
+    flip(0)
+    multiply(0)
+    pick_up(1)
+    flip(1)
+    for i in range(1, 8):
+        if i < 7:
+            pick_up(i + 1)
+        multiply(i)
+        if i < 7:
+            flip(i + 1)
 
     lane = lax.broadcasted_iota(jnp.int32, (32, 128), 1)
     line = lax.broadcasted_iota(jnp.int32, (32, 128), 0)
@@ -207,8 +193,8 @@
     step = 2 * (dr + 1) + jnp.where(dc < 0, 1, 0)
     slot = jnp.where(
         dc == 0,
-        jnp.where(dr == 0, 0, jnp.where(dr < 0, 5, 6)),
-        1 + step + jnp.where(dr > 0, 2, 0),
+        jnp.where(dr == 0, OWN_SLOT, jnp.where(dr < 0, 2, 3)),
+        step + jnp.where(step >= 2, 3, 0),
     )
     good = (turn != 2) & (to_col >= 0) & (to_col < NCOL) & (dr >= -1) & (dr <= 1)
     place = jnp.where(good, (to_col // NZ) * 9 + slot, EMPTY)
@@ -227,51 +213,47 @@
     column = lax.broadcasted_iota(jnp.int32, (NCOL, WIDE), 0)
     near = (jnp.abs(mine_col - column) <= 1) & (jnp.abs(mine_row - row) <= 1)
 
+    mask_out[...] = jnp.where(near, 1.0, 0.0)
     held[EMPTY] = jnp.zeros((HALF, 128), f32)
 
-    for copy in land_copies:
-        copy.wait()
-
+    land_copy.wait()
     final = lax.broadcasted_iota(jnp.int32, (K, 128), 1) == 127
 
-    def land_two(t, total):
-        for odd in (0, 1):
-            gather_rows(cells, land_idx, pair_step(t, odd)[2] * ROWS, landed.at[2 * t + odd])
-        x0 = t * 32
+    def land(t):
+        for i in (2 * t, 2 * t + 1):
+            gather_rows(cells, land_idx, direction(i), landed.at[i])
+
+    def gram(x0):
         left, right = [], []
-        for v in range(32):
-            z = zlines[x0 + v]
-            beside = zlines[x0 + v + 1] + jnp.where(final, 0.0, pltpu.roll(z, 127, 1))
-            half_image = (2.0 + 0.5 * coef[0, 0, pl.ds(x0 + v, 1), :]) * z - beside
-            left.append(zparts[x0 + v])
+        for x in range(x0, x0 + CX // 4):
+            z = zlines[x]
+            beside = zlines[x + 1] + jnp.where(final, 0.0, pltpu.roll(z, 127, 1))
+            half_image = (2.0 + 0.5 * coef[0, 0, x : x + 1, :]) * z - beside
+            left.append(zparts[x])
             right.append(stacked(half_image))
-        return total + lax.dot_general(
+        return lax.dot_general(
             jnp.concatenate(left, axis=1),
             jnp.concatenate(right, axis=1),
             (((1,), (1,)), ((), ())),
             preferred_element_type=f32,
         )
 
-    own = unstack(lax.fori_loop(0, 4, land_two, jnp.zeros((2 * K, 2 * K), f32)))
-    own = own + own.T
-
     def put(slot, block):
         gap = jnp.zeros((HALF, 64 - K), f32)
         held[x_me * 9 + slot] = jnp.concatenate([block[:HALF], gap, block[HALF:], gap], axis=1)
 
-    def x_copy(t, k):
-        span = pl.ds(x_me * 9 + (2 * t + 1 if t else 0), 2 if t else 3)
+    def x_copy(g, k):
+        span = pl.ds(x_me * 9 + GROUPS[g][0], GROUPS[g][1])
         return pltpu.make_async_remote_copy(
             src_ref=held.at[span],
             dst_ref=held.at[span],
-            send_sem=x_send.at[t * 3 + k - 1],
-            recv_sem=x_recv.at[t * 3 + k - 1],
+            send_sem=x_send.at[g * 3 + k - 1],
+            recv_sem=x_recv.at[g * 3 + k - 1],
             device_id=(row, lax.rem(col + NZ * k, NCOL)),
             device_id_type=MESH,
         )
 
-    put(0, own)
-    for t in FINISH:
+    def pair(t):
         for i in (2 * t, 2 * t + 1):
             dr, dc = STEPS[i]
             if remote:
@@ -281,10 +263,31 @@
             product = jnp.dot(
                 stacked(arrived[i]), landed[i].astype(bf16), preferred_element_type=f32
             )
-            put(i + 1, unstack(product.T))
+            put(SLOTS[i], unstack(product.T))
+
+    def send_along_x(g):
         if remote:
             for k in (2, 1, 3):
-                x_copy(t, k).start()
+                x_copy(g, k).start()
+
+    land(0)
+    own = gram(0)
+    land(2)
+    own += gram(CX // 4)
+    pair(0)
+    send_along_x(0)
+    land(1)
+    own += gram(CX // 2)
+    pair(2)
+    send_along_x(1)
+    land(3)
+    own += gram(3 * CX // 4)
+    own = unstack(own)
+    put(OWN_SLOT, own + own.T)
+    pair(1)
+    send_along_x(2)
+    pair(3)
+    send_along_x(3)
 
     pick_copy.wait()
     if remote:
@@ -327,8 +330,13 @@
             z_copy(k).wait_send()
         for k in range(1, 4):
             z_copy(k).wait_recv()
+    strips_out[...] = received[...]
+
+
+def place_strips(strips, mask, out):
     for p in range(NCOL):
-        out[p * K : (p + 1) * K, :] = jnp.where(near[p : p + 1, :], received[p % NZ], 0.0)
+        keep = mask[p : p + 1, :] > 0.5
+        out[p * K : (p + 1) * K, :] = jnp.where(keep, strips[p % NZ], 0.0)
 
 
 def assemble_call(remote, *args):
@@ -338,9 +346,12 @@
     dma = pltpu.SemaphoreType.DMA
     return pl.pallas_call(
         functools.partial(assemble, remote),
-        out_shape=jax.ShapeDtypeStruct((NCOL * K, WIDE), f32),
+        out_shape=(
+            jax.ShapeDtypeStruct((NZ, K, WIDE), f32),
+            jax.ShapeDtypeStruct((NCOL, WIDE), f32),
+        ),
         in_specs=[hbm, vmem, hbm, hbm, hbm, smem, vmem],
-        out_specs=vmem,
+        out_specs=(vmem, vmem),
         scratch_shapes=[
             pltpu.VMEM((CX + 1, K, 128), f32),
             pltpu.VMEM((CX, 2 * K, 128), bf16),
@@ -348,6 +359,8 @@
             pltpu.VMEM((8, ROWS, ROWS), f32),
             pltpu.VMEM((ROWS, 128), f32),
             pltpu.VMEM((ROWS, 128), f32),
+            pltpu.VMEM((2 * K, ROWS), bf16),
+            pltpu.VMEM((2 * K, ROWS), bf16),
             pltpu.VMEM((8, ROWS, 128), f32),
             pltpu.VMEM((8, K, ROWS), f32),
             pltpu.VMEM((8, K, ROWS), f32),
@@ -355,10 +368,10 @@
             pltpu.VMEM((NZ, K, WIDE), f32),
             pltpu.VMEM((NZ, K, WIDE), f32),
             pltpu.VMEM((32, 128), jnp.int32),
-            pltpu.SMEM((8 * ROWS,), jnp.int32),
-            pltpu.SMEM((8 * ROWS,), jnp.int32),
+            pltpu.SMEM((8, ROWS), jnp.int32),
+            pltpu.SMEM((8, ROWS), jnp.int32),
             pltpu.SMEM((32, 128), jnp.int32),
-            dma((HALVES,)), dma((8,)), dma((8,)), dma((8,)), dma,
+            dma((HALVES,)), dma((8,)), dma, dma, dma,
             dma((8,)), dma((8,)), dma((12,)), dma((12,)), dma((3,)), dma((3,)),
         ],
         compiler_params=pltpu.CompilerParams(
@@ -373,7 +386,13 @@
 
 
 def on_device(zvecs, coef, blocks, send_idx, land_idx, active, order):
-    return assemble_call(True, zvecs, coef, blocks, send_idx, land_idx, active, order)
+    strips, mask = assemble_call(True, zvecs, coef, blocks, send_idx, land_idx, active, order)
+    return pl.pallas_call(
+        place_strips,
+        out_shape=jax.ShapeDtypeStruct((NCOL * K, WIDE), f32),
+        in_specs=[pl.BlockSpec(memory_space=pltpu.VMEM)] * 2,
+        out_specs=pl.BlockSpec(memory_space=pltpu.VMEM),
+    )(strips, mask)
 
 
 def solution(mesh):

time: 40.3 us -> 37.5 us (0.931)
  local copies, waits for them, and re-layouts: 2.36 us -> 0 us
  Pallas kernels: 37.6 us -> 36.9 us
    unnamed x1 -> x0, local copies, waits for them, and re-layouts: 2.36 us -> none
    pallas_call x1 -> x2, Pallas kernels: 37.6 us -> 36.9 us  [the longest x1 34.9 us: assemble_call(): pl.pallas_call(functools.partial(assemble, remote), out_shape=(jax.ShapeD...]
where the time goes in v3:
time: 37.5 us; the launch traced here: 36.9 us
  Pallas kernels  36.9 us (98%)
    pallas_call x1, Pallas kernels, assemble_call(): pl.pallas_call(functools.partial(assemble, remote), out_shape=(jax.ShapeD...  34.9 us
    pallas_call x1, Pallas kernels, on_device(): pl.pallas_call(place_strips, out_shape=jax.ShapeDtypeStruct((NCOL * K, WI...  2.07 us

profile of v3, /device:TPU:8, one launch (start us, length us, event | category | flops | bytes accessed | tf_op | source)
XLA Modules:
  0.0 36.9 jit_solution(8969214828791569145)
XLA Ops:
  0.0 34.9 %shard_map.73 = (f32[4,48,384]{2,1,0:T(8,128)}, f32[16,384]{1,0:T(8,128)}) custom-call(f32[1,1,48,128,128]{4,3,2,1,0:T(8,128)} %z_hbm.1, f32[1,1,128,128]{3,2,1,0:T(8,128)} %coef.1, f32[1,1,8,640,640]{4,3,2,1,0:T(8,128)} %blocks_hbm.1, s32[1,1,8,640]{3,2,1,0:T(8,128)} %send_hbm.1, s32[1,1,8,640]{3,2,1,0:T(8,128)} %land_hbm.1, s32[1,1,8]{2,1,0:T(1,128)} %active.1, ...), custom_call_target="tpu_custom_call" | custom-call | flops 2000000000 | bytes 18000000 | tf_op jit(solution)/shard_map/pallas_call | solution.py:347
  34.9 2.1 %shard_map.74 = f32[768,384]{1,0:T(8,128)} custom-call(f32[4,48,384]{2,1,0:T(8,128)} %get-tuple-element.7.strips, f32[16,384]{1,0:T(8,128)} %get-tuple-element.8.mask), custom_call_target="tpu_custom_call" | custom-call | tf_op jit(solution)/shard_map/pallas_call | solution.py:390

commit v4 on v3

--- a/solution.py
+++ b/solution.py
@@ -48,12 +48,19 @@
     return nine - nine // 5
 
 
-def gather_rows(cells, index, n, rows):
+def gathering(cells, index, n, rows, batch):
     for j in range(ROWS):
         rows[pl.ds(j, 1), :] = cells[pl.ds(index[n, j], 1), :]
-
-
-def times_block(picked, block, factor, out):
+        if j % batch == batch - 1:
+            yield
+
+
+def finish(steps):
+    for _ in steps:
+        pass
+
+
+def times_block(picked, block, factor, out, beside):
     for q0 in range(0, ROWS, 256):
         q1 = min(q0 + 256, ROWS)
         total, low_total = None, None
@@ -64,17 +71,19 @@
             two = jnp.dot(picked[0:K, p0:p1], low, preferred_element_type=f32)
             total = one if total is None else total + one
             low_total = two if low_total is None else low_total + two
+            next(beside, None)
         out[:, q0:q1] = (total[0:K] + total[K : 2 * K] + low_total) * factor
+    finish(beside)
 
 
 def assemble(
     remote,
-    z_hbm, coef, blocks_hbm, send_hbm, land_hbm, active, order,
+    z_hbm, coef_hbm, blocks_hbm, send_hbm, land_hbm, active_hbm, order_hbm,
     strips_out, mask_out,
     zlines, zparts, cells, blocks, rows_a, rows_b, picked_a, picked_b, landed, sent, arrived,
-    held, strips, received,
-    pick_vec, send_idx, land_idx, pick,
-    z_sem, block_sem, send_idx_sem, land_idx_sem, pick_sem,
+    held, strips, received, coef, order,
+    pick_vec, send_idx, land_idx, active, pick,
+    z_sem, block_sem, send_idx_sem, land_idx_sem, small_sem, pick_sem,
     near_send, near_recv, x_send, x_recv, z_send, z_recv,
 ):
     row = lax.axis_index("row") if remote else 3
@@ -85,6 +94,8 @@
     def lines_of(half):
         return zlines.at[pl.ds(half * PER, PER)]
 
+    send_copy = pltpu.make_async_copy(send_hbm.at[0, 0], send_idx, send_idx_sem)
+    send_copy.start()
     for half in range(HALVES):
         for k in range(K):
             pltpu.make_async_copy(
@@ -92,16 +103,15 @@
                 zlines.at[pl.ds(half * PER, PER), k, :],
                 z_sem.at[half],
             ).start()
-    send_copy = pltpu.make_async_copy(send_hbm.at[0, 0], send_idx, send_idx_sem)
-    send_copy.start()
+    active_copy = pltpu.make_async_copy(active_hbm.at[0], active, small_sem.at[0])
+    active_copy.start()
+    coef_copy = pltpu.make_async_copy(coef_hbm.at[0, 0], coef, small_sem.at[1])
+    order_copy = pltpu.make_async_copy(order_hbm, order, small_sem.at[2])
+    land_copy = pltpu.make_async_copy(land_hbm.at[0, 0], land_idx, land_idx_sem)
     block_copies = [
         pltpu.make_async_copy(blocks_hbm.at[0, 0, direction(i)], blocks.at[i], block_sem.at[i])
         for i in range(8)
     ]
-    for copy in block_copies:
-        copy.start()
-    land_copy = pltpu.make_async_copy(land_hbm.at[0, 0], land_idx, land_idx_sem)
-    land_copy.start()
 
     if remote:
         barrier = pltpu.get_barrier_semaphore()
@@ -124,9 +134,13 @@
 
     for half in range(HALVES):
         pltpu.make_async_copy(lines_of(half), lines_of(half), z_sem.at[half]).wait()
+        if half == HALVES - 1:
+            for copy in block_copies + [order_copy, coef_copy, land_copy]:
+                copy.start()
         lax.fori_loop(half * PER // TURN, (half + 1) * PER // TURN, turn_chunk, 0)
 
     send_copy.wait()
+    active_copy.wait()
 
     if remote:
         pl.semaphore_wait(barrier, 14)
@@ -150,15 +164,15 @@
     picked = (picked_a, picked_b)
 
     def pick_up(i):
-        gather_rows(cells, send_idx, direction(i), rows[i % 2])
+        return gathering(cells, send_idx, direction(i), rows[i % 2], 72)
 
     def flip(i):
         picked[i % 2][...] = rows[i % 2][...].astype(bf16).T[0 : 2 * K]
 
-    def multiply(i):
+    def multiply(i, beside=iter(())):
         block_copies[i].wait()
-        keep = jnp.where(active[0, 0, direction(i)] == 1, 1.0, 0.0)
-        times_block(picked[i % 2], blocks.at[i], keep, sent.at[i])
+        keep = jnp.where(active[0, direction(i)] == 1, 1.0, 0.0)
+        times_block(picked[i % 2], blocks.at[i], keep, sent.at[i], beside)
         if remote:
             dr, dc = STEPS[i]
 
@@ -166,18 +180,17 @@
             def _():
                 near_copy(i, dr, dc).start()
 
-    pick_up(0)
+    finish(pick_up(0))
     flip(0)
     multiply(0)
-    pick_up(1)
+    finish(pick_up(1))
     flip(1)
-    for i in range(1, 8):
-        if i < 7:
-            pick_up(i + 1)
-        multiply(i)
-        if i < 7:
-            flip(i + 1)
-
+    for i in range(1, 7):
+        multiply(i, pick_up(i + 1))
+        flip(i + 1)
+    multiply(7)
+
+    order_copy.wait()
     lane = lax.broadcasted_iota(jnp.int32, (32, 128), 1)
     line = lax.broadcasted_iota(jnp.int32, (32, 128), 0)
     owner = order[...].reshape(1, 128)
@@ -217,26 +230,32 @@
     held[EMPTY] = jnp.zeros((HALF, 128), f32)
 
     land_copy.wait()
+    coef_copy.wait()
     final = lax.broadcasted_iota(jnp.int32, (K, 128), 1) == 127
 
-    def land(t):
-        for i in (2 * t, 2 * t + 1):
-            gather_rows(cells, land_idx, direction(i), landed.at[i])
-
-    def gram(x0):
-        left, right = [], []
-        for x in range(x0, x0 + CX // 4):
-            z = zlines[x]
-            beside = zlines[x + 1] + jnp.where(final, 0.0, pltpu.roll(z, 127, 1))
-            half_image = (2.0 + 0.5 * coef[0, 0, x : x + 1, :]) * z - beside
-            left.append(zparts[x])
-            right.append(stacked(half_image))
-        return lax.dot_general(
-            jnp.concatenate(left, axis=1),
-            jnp.concatenate(right, axis=1),
-            (((1,), (1,)), ((), ())),
-            preferred_element_type=f32,
+    def land(t, x0, total):
+        beside = (
+            step
+            for i in (2 * t, 2 * t + 1)
+            for step in gathering(cells, land_idx, direction(i), landed.at[i], 80)
         )
+        for x in range(x0, x0 + CX // 4, 2):
+            left, right = [], []
+            for y in (x, x + 1):
+                z = zlines[y]
+                shifted = zlines[y + 1] + jnp.where(final, 0.0, pltpu.roll(z, 127, 1))
+                half_image = (2.0 + 0.5 * coef[y : y + 1, :]) * z - shifted
+                left.append(zparts[y])
+                right.append(stacked(half_image))
+            total = total + lax.dot_general(
+                jnp.concatenate(left, axis=1),
+                jnp.concatenate(right, axis=1),
+                (((1,), (1,)), ((), ())),
+                preferred_element_type=f32,
+            )
+            next(beside, None)
+        finish(beside)
+        return total
 
     def put(slot, block):
         gap = jnp.zeros((HALF, 64 - K), f32)
@@ -270,18 +289,14 @@
             for k in (2, 1, 3):
                 x_copy(g, k).start()
 
-    land(0)
-    own = gram(0)
-    land(2)
-    own += gram(CX // 4)
+    own = land(0, 0, jnp.zeros((2 * K, 2 * K), f32))
+    own = land(2, CX // 4, own)
     pair(0)
     send_along_x(0)
-    land(1)
-    own += gram(CX // 2)
+    own = land(1, CX // 2, own)
     pair(2)
     send_along_x(1)
-    land(3)
-    own += gram(3 * CX // 4)
+    own = land(3, 3 * CX // 4, own)
     own = unstack(own)
     put(OWN_SLOT, own + own.T)
     pair(1)
@@ -341,7 +356,6 @@
 
 def assemble_call(remote, *args):
     vmem = pl.BlockSpec(memory_space=pltpu.VMEM)
-    smem = pl.BlockSpec(memory_space=pltpu.SMEM)
     hbm = pl.BlockSpec(memory_space=pl.ANY)
     dma = pltpu.SemaphoreType.DMA
     return pl.pallas_call(
@@ -350,7 +364,7 @@
             jax.ShapeDtypeStruct((NZ, K, WIDE), f32),
             jax.ShapeDtypeStruct((NCOL, WIDE), f32),
         ),
-        in_specs=[hbm, vmem, hbm, hbm, hbm, smem, vmem],
+        in_specs=[hbm] * 7,
         out_specs=(vmem, vmem),
         scratch_shapes=[
             pltpu.VMEM((CX + 1, K, 128), f32),
@@ -367,11 +381,14 @@
             pltpu.VMEM((EMPTY + 1, HALF, 128), f32),
             pltpu.VMEM((NZ, K, WIDE), f32),
             pltpu.VMEM((NZ, K, WIDE), f32),
+            pltpu.VMEM((CX, 128), f32),
+            pltpu.VMEM((128,), jnp.int32),
             pltpu.VMEM((32, 128), jnp.int32),
             pltpu.SMEM((8, ROWS), jnp.int32),
             pltpu.SMEM((8, ROWS), jnp.int32),
+            pltpu.SMEM((1, 8), jnp.int32),
             pltpu.SMEM((32, 128), jnp.int32),
-            dma((HALVES,)), dma((8,)), dma, dma, dma,
+            dma((HALVES,)), dma((8,)), dma, dma, dma((3,)), dma,
             dma((8,)), dma((8,)), dma((12,)), dma((12,)), dma((3,)), dma((3,)),
         ],
         compiler_params=pltpu.CompilerParams(

time: 37.5 us -> 33.1 us (0.88); the launches traced: 36.9 us -> 32.9 us
  Pallas kernels: 36.9 us -> 32.9 us
    pallas_call x1, Pallas kernels: 34.9 us -> 30.9 us  [assemble_call(): pl.pallas_call(functools.partial(assemble, remote), out_shape=(jax.ShapeD...]
where the time goes in v4:
time: 33.1 us; the launch traced here: 32.9 us
  Pallas kernels  32.9 us (99%)
    pallas_call x1, Pallas kernels, assemble_call(): pl.pallas_call(functools.partial(assemble, remote), out_shape=(jax.ShapeD...  30.9 us
    pallas_call x1, Pallas kernels, on_device(): pl.pallas_call(place_strips, out_shape=jax.ShapeDtypeStruct((NCOL * K, WI...  2.07 us

profile of v4, /device:TPU:8, one launch (start us, length us, event | category | flops | bytes accessed | tf_op | source)
XLA Modules:
  0.0 32.9 jit_solution(17014793813191851410)
XLA Ops:
  0.0 30.9 %shard_map.73 = (f32[4,48,384]{2,1,0:T(8,128)}, f32[16,384]{1,0:T(8,128)}) custom-call(f32[1,1,48,128,128]{4,3,2,1,0:T(8,128)} %z_hbm.1, f32[1,1,128,128]{3,2,1,0:T(8,128)} %coef_hbm.1, f32[1,1,8,640,640]{4,3,2,1,0:T(8,128)} %blocks_hbm.1, s32[1,1,8,640]{3,2,1,0:T(8,128)} %send_hbm.1, s32[1,1,8,640]{3,2,1,0:T(8,128)} %land_hbm.1, s32[1,1,8]{2,1,0:T(1,128)} %active_hbm.1, ...), custom_call_target="tpu_custom_call" | custom-call | flops 2000000000 | bytes 18000000 | tf_op jit(solution)/shard_map/pallas_call | solution.py:361
  30.9 2.1 %shard_map.74 = f32[768,384]{1,0:T(8,128)} custom-call(f32[4,48,384]{2,1,0:T(8,128)} %get-tuple-element.7.strips, f32[16,384]{1,0:T(8,128)} %get-tuple-element.8.mask), custom_call_target="tpu_custom_call" | custom-call | tf_op jit(solution)/shard_map/pallas_call | solution.py:407

commit v5 on v4

--- a/solution.py
+++ b/solution.py
@@ -18,8 +18,8 @@
 NCOL = 16
 NX = 4
 NZ = 4
-HALVES = 2
-PER = CX // HALVES
+PARTS = 2
+PER = CX // PARTS
 TURN = 32
 HALF = K // 2
 WIDE = 8 * K
@@ -81,9 +81,9 @@
     z_hbm, coef_hbm, blocks_hbm, send_hbm, land_hbm, active_hbm, order_hbm,
     strips_out, mask_out,
     zlines, zparts, cells, blocks, rows_a, rows_b, picked_a, picked_b, landed, sent, arrived,
-    held, strips, received, coef, order,
+    held, strips, mask, coef, order,
     pick_vec, send_idx, land_idx, active, pick,
-    z_sem, block_sem, send_idx_sem, land_idx_sem, small_sem, pick_sem,
+    z_sem, block_sem, send_idx_sem, land_idx_sem, small_sem, pick_sem, out_sem,
     near_send, near_recv, x_send, x_recv, z_send, z_recv,
 ):
     row = lax.axis_index("row") if remote else 3
@@ -91,17 +91,17 @@
     x_me = col // NZ
     z_me = lax.rem(col, NZ)
 
-    def lines_of(half):
-        return zlines.at[pl.ds(half * PER, PER)]
+    def lines_of(part):
+        return zlines.at[pl.ds(part * PER, PER)]
 
     send_copy = pltpu.make_async_copy(send_hbm.at[0, 0], send_idx, send_idx_sem)
     send_copy.start()
-    for half in range(HALVES):
+    for part in range(PARTS):
         for k in range(K):
             pltpu.make_async_copy(
-                z_hbm.at[0, 0, k, pl.ds(half * PER, PER), :],
-                zlines.at[pl.ds(half * PER, PER), k, :],
-                z_sem.at[half],
+                z_hbm.at[0, 0, k, pl.ds(part * PER, PER), :],
+                zlines.at[pl.ds(part * PER, PER), k, :],
+                z_sem.at[part],
             ).start()
     active_copy = pltpu.make_async_copy(active_hbm.at[0], active, small_sem.at[0])
     active_copy.start()
@@ -132,12 +132,12 @@
             cells[pl.ds((i * TURN + u) * 128, 128), 0 : 2 * K] = both.T.astype(f32)
         return carry
 
-    for half in range(HALVES):
-        pltpu.make_async_copy(lines_of(half), lines_of(half), z_sem.at[half]).wait()
-        if half == HALVES - 1:
+    for part in range(PARTS):
+        pltpu.make_async_copy(lines_of(part), lines_of(part), z_sem.at[part]).wait()
+        if part == PARTS - 1:
             for copy in block_copies + [order_copy, coef_copy, land_copy]:
                 copy.start()
-        lax.fori_loop(half * PER // TURN, (half + 1) * PER // TURN, turn_chunk, 0)
+        lax.fori_loop(part * PER // TURN, (part + 1) * PER // TURN, turn_chunk, 0)
 
     send_copy.wait()
     active_copy.wait()
@@ -226,7 +226,9 @@
     column = lax.broadcasted_iota(jnp.int32, (NCOL, WIDE), 0)
     near = (jnp.abs(mine_col - column) <= 1) & (jnp.abs(mine_row - row) <= 1)
 
-    mask_out[...] = jnp.where(near, 1.0, 0.0)
+    mask[...] = jnp.where(near, 1.0, 0.0)
+    mask_copy = pltpu.make_async_copy(mask, mask_out, out_sem.at[0])
+    mask_copy.start()
     held[EMPTY] = jnp.zeros((HALF, 128), f32)
 
     land_copy.wait()
@@ -313,7 +315,7 @@
     def z_copy(k):
         return pltpu.make_async_remote_copy(
             src_ref=strips.at[k],
-            dst_ref=received.at[z_me],
+            dst_ref=strips_out.at[z_me],
             send_sem=z_send.at[k - 1],
             recv_sem=z_recv.at[k - 1],
             device_id=(row, x_me * NZ + lax.rem(z_me + k, NZ)),
@@ -326,12 +328,11 @@
         upper = jnp.concatenate([block[:, 0:K] for block in found], axis=1)
         lower = jnp.concatenate([block[:, 64 : 64 + K] for block in found], axis=1)
         strip = jnp.concatenate([upper, lower], axis=0)
-        if k:
-            strips[k] = strip
-            if remote:
-                z_copy(k).start()
-        else:
-            received[z_me] = strip
+        strips[k] = strip
+        if k and remote:
+            z_copy(k).start()
+    own_copy = pltpu.make_async_copy(strips.at[0], strips_out.at[z_me], out_sem.at[1])
+    own_copy.start()
 
     if remote:
         for i, (dr, dc) in enumerate(STEPS):
@@ -345,7 +346,8 @@
             z_copy(k).wait_send()
         for k in range(1, 4):
             z_copy(k).wait_recv()
-    strips_out[...] = received[...]
+    mask_copy.wait()
+    own_copy.wait()
 
 
 def place_strips(strips, mask, out):
@@ -355,7 +357,6 @@
 
 
 def assemble_call(remote, *args):
-    vmem = pl.BlockSpec(memory_space=pltpu.VMEM)
     hbm = pl.BlockSpec(memory_space=pl.ANY)
     dma = pltpu.SemaphoreType.DMA
     return pl.pallas_call(
@@ -365,7 +366,7 @@
             jax.ShapeDtypeStruct((NCOL, WIDE), f32),
         ),
         in_specs=[hbm] * 7,
-        out_specs=(vmem, vmem),
+        out_specs=(hbm, hbm),
         scratch_shapes=[
             pltpu.VMEM((CX + 1, K, 128), f32),
             pltpu.VMEM((CX, 2 * K, 128), bf16),
@@ -380,7 +381,7 @@
             pltpu.VMEM((8, K, ROWS), f32),
             pltpu.VMEM((EMPTY + 1, HALF, 128), f32),
             pltpu.VMEM((NZ, K, WIDE), f32),
-            pltpu.VMEM((NZ, K, WIDE), f32),
+            pltpu.VMEM((NCOL, WIDE), f32),
             pltpu.VMEM((CX, 128), f32),
             pltpu.VMEM((128,), jnp.int32),
             pltpu.VMEM((32, 128), jnp.int32),
@@ -388,7 +389,7 @@
             pltpu.SMEM((8, ROWS), jnp.int32),
             pltpu.SMEM((1, 8), jnp.int32),
             pltpu.SMEM((32, 128), jnp.int32),
-            dma((HALVES,)), dma((8,)), dma, dma, dma((3,)), dma,
+            dma((PARTS,)), dma((8,)), dma, dma, dma((3,)), dma, dma((2,)),
             dma((8,)), dma((8,)), dma((12,)), dma((12,)), dma((3,)), dma((3,)),
         ],
         compiler_params=pltpu.CompilerParams(

time: 33.1 us -> 32.6 us (0.985)
  Pallas kernels: 32.9 us -> 32.4 us
    pallas_call x1, Pallas kernels: 30.9 us -> 30.3 us  [assemble_call(): pl.pallas_call(functools.partial(assemble, remote), out_shape=(jax.ShapeD...]
where the time goes in v5:
time: 32.6 us; the launch traced here: 32.4 us
  Pallas kernels  32.4 us (99%)
    pallas_call x1, Pallas kernels, assemble_call(): pl.pallas_call(functools.partial(assemble, remote), out_shape=(jax.ShapeD...  30.3 us
    pallas_call x1, Pallas kernels, on_device(): pl.pallas_call(place_strips, out_shape=jax.ShapeDtypeStruct((NCOL * K, WI...  2.07 us

profile of v5, /device:TPU:8, one launch (start us, length us, event | category | flops | bytes accessed | tf_op | source)
XLA Modules:
  0.0 32.4 jit_solution(15498030752923861058)
XLA Ops:
  0.0 30.3 %shard_map.73 = (f32[4,48,384]{2,1,0:T(8,128)}, f32[16,384]{1,0:T(8,128)}) custom-call(f32[1,1,48,128,128]{4,3,2,1,0:T(8,128)} %z_hbm.1, f32[1,1,128,128]{3,2,1,0:T(8,128)} %coef_hbm.1, f32[1,1,8,640,640]{4,3,2,1,0:T(8,128)} %blocks_hbm.1, s32[1,1,8,640]{3,2,1,0:T(8,128)} %send_hbm.1, s32[1,1,8,640]{3,2,1,0:T(8,128)} %land_hbm.1, s32[1,1,8]{2,1,0:T(1,128)} %active_hbm.1, ...), custom_call_target="tpu_custom_call" | custom-call | flops 2000000000 | bytes 18000000 | tf_op jit(solution)/shard_map/pallas_call | solution.py:362
  30.4 2.1 %shard_map.74 = f32[768,384]{1,0:T(8,128)} custom-call(f32[4,48,384]{2,1,0:T(8,128)} %get-tuple-element.7.strips, f32[16,384]{1,0:T(8,128)} %get-tuple-element.8.mask), custom_call_target="tpu_custom_call" | custom-call | tf_op jit(solution)/shard_map/pallas_call | solution.py:408

commit v6 on v5

--- a/solution.py
+++ b/solution.py
@@ -189,6 +189,81 @@
         multiply(i, pick_up(i + 1))
         flip(i + 1)
     multiply(7)
+
+    land_copy.wait()
+    coef_copy.wait()
+    final = lax.broadcasted_iota(jnp.int32, (K, 128), 1) == 127
+
+    def land(t, x0, total):
+        beside = (
+            step
+            for i in (2 * t, 2 * t + 1)
+            for step in gathering(cells, land_idx, direction(i), landed.at[i], 80)
+        )
+        for x in range(x0, x0 + CX // 4, 2):
+            left, right = [], []
+            for y in (x, x + 1):
+                z = zlines[y]
+                shifted = zlines[y + 1] + jnp.where(final, 0.0, pltpu.roll(z, 127, 1))
+                half_image = (2.0 + 0.5 * coef[y : y + 1, :]) * z - shifted
+                left.append(zparts[y])
+                right.append(stacked(half_image))
+            total = total + lax.dot_general(
+                jnp.concatenate(left, axis=1),
+                jnp.concatenate(right, axis=1),
+                (((1,), (1,)), ((), ())),
+                preferred_element_type=f32,
+            )
+            next(beside, None)
+        finish(beside)
+        return total
+
+    def put(slot, block):
+        gap = jnp.zeros((HALF, 64 - K), f32)
+        held[x_me * 9 + slot] = jnp.concatenate([block[:HALF], gap, block[HALF:], gap], axis=1)
+
+    def x_copy(g, k):
+        span = pl.ds(x_me * 9 + GROUPS[g][0], GROUPS[g][1])
+        return pltpu.make_async_remote_copy(
+            src_ref=held.at[span],
+            dst_ref=held.at[span],
+            send_sem=x_send.at[g * 3 + k - 1],
+            recv_sem=x_recv.at[g * 3 + k - 1],
+            device_id=(row, lax.rem(col + NZ * k, NCOL)),
+            device_id_type=MESH,
+        )
+
+    def pair(t):
+        for i in (2 * t, 2 * t + 1):
+            dr, dc = STEPS[i]
+            if remote:
+                @pl.when(inside(-dr, -dc))
+                def _():
+                    near_copy(i, dr, dc).wait_recv()
+            product = jnp.dot(
+                stacked(arrived[i]), landed[i].astype(bf16), preferred_element_type=f32
+            )
+            put(SLOTS[i], unstack(product.T))
+
+    def send_along_x(g):
+        if remote:
+            for k in (2, 1, 3):
+                x_copy(g, k).start()
+
+    own = land(0, 0, jnp.zeros((2 * K, 2 * K), f32))
+    own = land(2, CX // 4, own)
+    pair(0)
+    send_along_x(0)
+    own = land(1, CX // 2, own)
+    pair(2)
+    send_along_x(1)
+    own = land(3, 3 * CX // 4, own)
+    own = unstack(own)
+    put(OWN_SLOT, own + own.T)
+    pair(1)
+    send_along_x(2)
+    pair(3)
+    send_along_x(3)
 
     order_copy.wait()
     lane = lax.broadcasted_iota(jnp.int32, (32, 128), 1)
@@ -215,96 +290,7 @@
     pick_copy = pltpu.make_async_copy(pick_vec, pick, pick_sem)
     pick_copy.start()
 
-    lane8 = lax.broadcasted_iota(jnp.int32, (8, 128), 1)
-    line8 = lax.broadcasted_iota(jnp.int32, (8, 128), 0)
-    mine = jnp.sum(jnp.where(owner == col * 8 + line8, lane8, 0), axis=1, keepdims=True)
-    at = lax.broadcasted_iota(jnp.int32, (8, WIDE), 1) // K
-    here = at == lax.broadcasted_iota(jnp.int32, (8, WIDE), 0)
-    mine = jnp.sum(jnp.where(here, jnp.broadcast_to(mine, (8, WIDE)), 0), axis=0, keepdims=True)
-    mine_row = mine // NCOL
-    mine_col = mine - mine_row * NCOL
-    column = lax.broadcasted_iota(jnp.int32, (NCOL, WIDE), 0)
-    near = (jnp.abs(mine_col - column) <= 1) & (jnp.abs(mine_row - row) <= 1)
-
-    mask[...] = jnp.where(near, 1.0, 0.0)
-    mask_copy = pltpu.make_async_copy(mask, mask_out, out_sem.at[0])
-    mask_copy.start()
     held[EMPTY] = jnp.zeros((HALF, 128), f32)
-
-    land_copy.wait()
-    coef_copy.wait()
-    final = lax.broadcasted_iota(jnp.int32, (K, 128), 1) == 127
-
-    def land(t, x0, total):
-        beside = (
-            step
-            for i in (2 * t, 2 * t + 1)
-            for step in gathering(cells, land_idx, direction(i), landed.at[i], 80)
-        )
-        for x in range(x0, x0 + CX // 4, 2):
-            left, right = [], []
-            for y in (x, x + 1):
-                z = zlines[y]
-                shifted = zlines[y + 1] + jnp.where(final, 0.0, pltpu.roll(z, 127, 1))
-                half_image = (2.0 + 0.5 * coef[y : y + 1, :]) * z - shifted
-                left.append(zparts[y])
-                right.append(stacked(half_image))
-            total = total + lax.dot_general(
-                jnp.concatenate(left, axis=1),
-                jnp.concatenate(right, axis=1),
-                (((1,), (1,)), ((), ())),
-                preferred_element_type=f32,
-            )
-            next(beside, None)
-        finish(beside)
-        return total
-
-    def put(slot, block):
-        gap = jnp.zeros((HALF, 64 - K), f32)
-        held[x_me * 9 + slot] = jnp.concatenate([block[:HALF], gap, block[HALF:], gap], axis=1)
-
-    def x_copy(g, k):
-        span = pl.ds(x_me * 9 + GROUPS[g][0], GROUPS[g][1])
-        return pltpu.make_async_remote_copy(
-            src_ref=held.at[span],
-            dst_ref=held.at[span],
-            send_sem=x_send.at[g * 3 + k - 1],
-            recv_sem=x_recv.at[g * 3 + k - 1],
-            device_id=(row, lax.rem(col + NZ * k, NCOL)),
-            device_id_type=MESH,
-        )
-
-    def pair(t):
-        for i in (2 * t, 2 * t + 1):
-            dr, dc = STEPS[i]
-            if remote:
-                @pl.when(inside(-dr, -dc))
-                def _():
-                    near_copy(i, dr, dc).wait_recv()
-            product = jnp.dot(
-                stacked(arrived[i]), landed[i].astype(bf16), preferred_element_type=f32
-            )
-            put(SLOTS[i], unstack(product.T))
-
-    def send_along_x(g):
-        if remote:
-            for k in (2, 1, 3):
-                x_copy(g, k).start()
-
-    own = land(0, 0, jnp.zeros((2 * K, 2 * K), f32))
-    own = land(2, CX // 4, own)
-    pair(0)
-    send_along_x(0)
-    own = land(1, CX // 2, own)
-    pair(2)
-    send_along_x(1)
-    own = land(3, 3 * CX // 4, own)
-    own = unstack(own)
-    put(OWN_SLOT, own + own.T)
-    pair(1)
-    send_along_x(2)
-    pair(3)
-    send_along_x(3)
 
     pick_copy.wait()
     if remote:
@@ -334,6 +320,20 @@
     own_copy = pltpu.make_async_copy(strips.at[0], strips_out.at[z_me], out_sem.at[1])
     own_copy.start()
 
+    lane8 = lax.broadcasted_iota(jnp.int32, (8, 128), 1)
+    line8 = lax.broadcasted_iota(jnp.int32, (8, 128), 0)
+    mine = jnp.sum(jnp.where(owner == col * 8 + line8, lane8, 0), axis=1, keepdims=True)
+    at = lax.broadcasted_iota(jnp.int32, (8, WIDE), 1) // K
+    here = at == lax.broadcasted_iota(jnp.int32, (8, WIDE), 0)
+    mine = jnp.sum(jnp.where(here, jnp.broadcast_to(mine, (8, WIDE)), 0), axis=0, keepdims=True)
+    mine_row = mine // NCOL
+    mine_col = mine - mine_row * NCOL
+    column = lax.broadcasted_iota(jnp.int32, (NCOL, WIDE), 0)
+    near = (jnp.abs(mine_col - column) <= 1) & (jnp.abs(mine_row - row) <= 1)
+
+    mask[...] = jnp.where(near, 1.0, 0.0)
+    mask_copy = pltpu.make_async_copy(mask, mask_out, out_sem.at[0])
+    mask_copy.start()
     if remote:
         for i, (dr, dc) in enumerate(STEPS):
             @pl.when(inside(dr, dc))

time: 32.6 us -> 32.5 us (level)
  no operation moved by 1% of the time
where the time goes in v6:
time: 32.5 us; the launch traced here: 32.3 us
  Pallas kernels  32.3 us (99%)
    pallas_call x1, Pallas kernels, assemble_call(): pl.pallas_call(functools.partial(assemble, remote), out_shape=(jax.ShapeD...  30.2 us
    pallas_call x1, Pallas kernels, on_device(): pl.pallas_call(place_strips, out_shape=jax.ShapeDtypeStruct((NCOL * K, WI...  2.07 us

profile of v6, /device:TPU:8, one launch (start us, length us, event | category | flops | bytes accessed | tf_op | source)
XLA Modules:
  0.0 32.3 jit_solution(852177298272563056)
XLA Ops:
  0.0 30.2 %shard_map.73 = (f32[4,48,384]{2,1,0:T(8,128)}, f32[16,384]{1,0:T(8,128)}) custom-call(f32[1,1,48,128,128]{4,3,2,1,0:T(8,128)} %z_hbm.1, f32[1,1,128,128]{3,2,1,0:T(8,128)} %coef_hbm.1, f32[1,1,8,640,640]{4,3,2,1,0:T(8,128)} %blocks_hbm.1, s32[1,1,8,640]{3,2,1,0:T(8,128)} %send_hbm.1, s32[1,1,8,640]{3,2,1,0:T(8,128)} %land_hbm.1, s32[1,1,8]{2,1,0:T(1,128)} %active_hbm.1, ...), custom_call_target="tpu_custom_call" | custom-call | flops 2000000000 | bytes 18000000 | tf_op jit(solution)/shard_map/pallas_call | solution.py:362
  30.2 2.1 %shard_map.74 = f32[768,384]{1,0:T(8,128)} custom-call(f32[4,48,384]{2,1,0:T(8,128)} %get-tuple-element.7.strips, f32[16,384]{1,0:T(8,128)} %get-tuple-element.8.mask), custom_call_target="tpu_custom_call" | custom-call | tf_op jit(solution)/shard_map/pallas_call | solution.py:408
